TPU v7x, 256 devices: a whole 4x4x8 slice. The times are simulated.
256 devices in a mesh: gx: 4 (over x_hi, core), gy: 4 (over y), gz: 16 (over x_lo, z).
Axes of the slice: x: 4 (x_hi: 2, x_lo: 2; x = x_hi * 2 + x_lo), y: 4, z: 8, core: 2. Of those that a mesh axis runs over, the one named last changes fastest.
Arguments:
- tokens: bfloat16 [1024, 6144], P(('gx', 'gy'), 'gz'), may hold values from -6 to 6
- w_up: bfloat16 [6144, 24576], P('gz', ('gx', 'gy')), may hold values from -0.109375 to 0.109375
- b_up: float32 [24576], P(('gx', 'gz')), may hold values from -3 to 3
- w_down: bfloat16 [24576, 6144], P(('gx', 'gy'), 'gz'), may hold values from -0.0546875 to 0.0546875
- b_down: float32 [6144], P('gz'), may hold values from -3 to 3
- cotangent: bfloat16 [1024, 6144], P(('gx', 'gy'), 'gz'), may hold values from -1.5 to 1.5
Outputs:
- output: bfloat16 [1024, 6144], P(('gx', 'gy'), 'gz')
- grad_tokens: bfloat16 [1024, 6144], P(('gx', 'gy'), 'gz')
- grad_w_up: bfloat16 [6144, 24576], P('gz', ('gx', 'gy'))
- grad_b_up: float32 [24576], P(('gx', 'gz'))
- grad_w_down: bfloat16 [24576, 6144], P(('gx', 'gy'), 'gz')
- grad_b_down: float32 [6144], P('gz')
All inputs are finite; a program needn't handle non-finite values.
Results may differ from a plain program's by a relative error of at most 0.033.
Values may be sent and summed in bfloat16 or wider, within the bound.
A program may use at most 128 MiB of HBM per device.

v0:
```python
import jax
import jax.numpy as jnp
from jax import lax
from jax.sharding import PartitionSpec as P

gelu_scale = 0.7978845608028654
gelu_cubic = 0.044715


def gelu_value(values):
    inner = gelu_scale * (values + gelu_cubic * values * values * values)
    return 0.5 * values * (1.0 + jnp.tanh(inner))


def gelu_slope(values):
    slope_tanh = jnp.tanh(gelu_scale * (values + gelu_cubic * values * values * values))
    return 0.5 * (1.0 + slope_tanh) + 0.5 * values * (
        1.0 - slope_tanh * slope_tanh
    ) * gelu_scale * (1.0 + 3.0 * gelu_cubic * values * values)


def contract_rows(left, right):
    return lax.dot_general(
        left, right, (((0,), (0,)), ((), ())), preferred_element_type=jnp.float32
    )


def contract_cols(left, right):
    return lax.dot_general(
        left, right, (((1,), (1,)), ((), ())), preferred_element_type=jnp.float32
    )


def per_device(tokens, w_up, b_up, w_down, b_down, cotangent):
    gathered = lax.all_gather(tokens, "gx", axis=0, tiled=True)
    up_block = lax.all_gather(w_up, "gy", axis=1, tiled=True)
    partial_pre = jnp.dot(gathered, up_block, preferred_element_type=jnp.float32)
    down_block = lax.all_gather(w_down, "gy", axis=0, tiled=True)
    pre_act = (
        lax.psum_scatter(
            partial_pre.astype(jnp.bfloat16), "gz", scatter_dimension=1, tiled=True
        ).astype(jnp.float32)
        + b_up[None, :]
    )
    act_full = lax.all_gather(gelu_value(pre_act).astype(jnp.bfloat16), "gz", axis=1, tiled=True)
    portion = act_full
    out_total = lax.psum_scatter(
        jnp.dot(portion, down_block, preferred_element_type=jnp.float32).astype(jnp.bfloat16),
        "gx",
        scatter_dimension=0,
        tiled=True,
    ).astype(jnp.float32)
    output = (out_total + b_down[None, :]).astype(jnp.bfloat16)
    cot_rows = lax.all_gather(cotangent, "gx", axis=0, tiled=True)
    partial_grad = contract_cols(cot_rows, down_block)
    grad_act = lax.psum_scatter(
        partial_grad.astype(jnp.bfloat16), "gz", scatter_dimension=1, tiled=True
    ).astype(jnp.float32)
    grad_own = (grad_act * gelu_slope(pre_act)).astype(jnp.bfloat16)
    grad_full = lax.all_gather(grad_own, "gz", axis=1, tiled=True)
    portion = act_full
    grad_w_down = lax.psum_scatter(
        contract_rows(portion, cot_rows).astype(jnp.bfloat16), "gy", scatter_dimension=0, tiled=True
    )
    portion = grad_full
    grad_tokens = lax.psum_scatter(
        contract_cols(portion, up_block).astype(jnp.bfloat16), "gx", scatter_dimension=0, tiled=True
    )
    up_partial = contract_rows(gathered, grad_full)
    grad_w_up = lax.psum_scatter(
        up_partial.astype(jnp.bfloat16), "gy", scatter_dimension=1, tiled=True
    )
    bias_up_local = jnp.sum(grad_own.astype(jnp.float32), axis=0)
    bias_down_local = jnp.sum(cot_rows.astype(jnp.float32), axis=0)
    grad_b_up, grad_b_down = lax.psum((bias_up_local, bias_down_local), "gy")
    return (output, grad_tokens, grad_w_up, grad_b_up, grad_w_down, grad_b_down)


def solution(mesh):
    placed = (
        P(("gx", "gy"), "gz"),
        P("gz", ("gx", "gy")),
        P(("gx", "gz")),
        P(("gx", "gy"), "gz"),
        P("gz"),
        P(("gx", "gy"), "gz"),
    )
    return jax.shard_map(
        per_device,
        mesh=mesh,
        in_specs=placed,
        out_specs=(
            P(("gx", "gy"), "gz"),
            P(("gx", "gy"), "gz"),
            P("gz", ("gx", "gy")),
            P(("gx", "gz")),
            P(("gx", "gy"), "gz"),
            P("gz"),
        ),
        check_vma=False,
    )
```

profile of v0, /device:TPU:1, one launch (start us, length us, event | category | flops | bytes accessed | tf_op | source)
XLA Modules:
  0.0 616.8 jit_solution(10049361228501025519)
XLA Ops:
  7.2 0.7 all-gather.5.cloned.1.call-update
  7.9 0.7 all-gather.9.cloned.1.call-update
  8.7 10.4 %all_gather.18 = bf16[256,384]{1,0:T(8,128)(2,1)S(1)} all-gather(bf16[64,384]{1,0:T(8,128)(2,1)} %param.6), channel_id=1, replica_groups=mesh['gx'=4,'gy'=4,'gz'=16] {'gx'}, dimensions={0}, use_global_device_ids=true | all-gather | bytes 245760 | tf_op jit(solution)/shard_map/all_gather | solution.py:35
  19.1 49.7 %all-gather.5.cloned.1.call-done = bf16[384,6144]{1,0:T(8,128)(2,1)} async-done(((bf16[384,1536]{1,0:T(8,128)(2,1)}), bf16[384,6144]{1,0:T(8,128)(2,1)}) %all-gather.5.cloned.1.call-update) | async-done | bytes 4718608 | tf_op jit(solution)/shard_map/all_gather | solution.py:36
  68.8 4.1 convolution_convert_fusion.3
  72.9 2.8 copy.14
  75.8 0.7 copy-done.1
  76.6 7.6 %all_gather.22 = bf16[256,384]{1,0:T(8,128)(2,1)S(1)} all-gather(bf16[64,384]{1,0:T(8,128)(2,1)S(1)} %copy-done.1), channel_id=1, replica_groups=mesh['gx'=4,'gy'=4,'gz'=16] {'gx'}, dimensions={0}, use_global_device_ids=true | all-gather | bytes 245760 | tf_op jit(solution)/shard_map/all_gather | solution.py:54
  84.2 42.1 %all-gather.9.cloned.1.call-done = bf16[6144,384]{1,0:T(8,128)(2,1)} async-done(((bf16[1536,384]{1,0:T(8,128)(2,1)}), bf16[6144,384]{1,0:T(8,128)(2,1)}) %all-gather.9.cloned.1.call-update) | async-done | bytes 4718608 | tf_op jit(solution)/shard_map/all_gather | solution.py:38
  126.3 4.2 convolution_convert_fusion.2
  130.5 2.9 copy.16
  133.4 0.0 all-gather.7.cloned.1.call-start
  133.4 63.4 %reduce-scatter.19.cloned.1.call-done = bf16[384,256]{1,0:T(8,128)(2,1)} async-done(((bf16[6144,256]{1,0:T(8,128)(2,1)}), bf16[384,256]{1,0:T(8,128)(2,1)}) %reduce-scatter.19.cloned.1.call-update) | async-done | bytes 196624
  196.9 1.1 copy.15
  197.9 75.9 %reduce-scatter.21.cloned.1.call-done = bf16[384,256]{1,0:T(8,128)(2,1)} async-done(((bf16[6144,256]{1,0:T(8,128)(2,1)}), bf16[384,256]{1,0:T(8,128)(2,1)}) %reduce-scatter.21.cloned.1.call-update) | async-done | bytes 196624
  273.8 1.1 copy.17
  274.9 1.1 convert_reduce_fusion.1
  276.1 0.5 all-gather.11.cloned.1.call-update
  276.7 70.5 %all-gather.7.cloned.1.call-done = bf16[256,6144]{1,0:T(8,128)(2,1)} async-done(((bf16[256,384]{1,0:T(8,128)(2,1)}), bf16[256,6144]{1,0:T(8,128)(2,1)}) %all-gather.7.cloned.1.call-update) | async-done | bytes 3145744 | tf_op jit(solution)/shard_map/all_gather | solution.py:45
  347.1 5.8 convolution_convert_fusion.5
  353.0 68.5 %all-gather.11.cloned.1.call-done = bf16[256,6144]{1,0:T(8,128)(2,1)} async-done(((bf16[256,384]{1,0:T(8,128)(2,1)}), bf16[256,6144]{1,0:T(8,128)(2,1)}) %all-gather.11.cloned.1.call-update) | async-done | bytes 3145744 | tf_op jit(solution)/shard_map/all_gather | solution.py:60
  421.5 5.9 fusion
  427.5 5.9 convolution_convert_fusion.4
  433.5 4.0 convolution_convert_fusion
  437.5 0.1 convert_reduce_fusion
  437.5 9.0 %all-reduce = (f32[384]{0:T(512)}, f32[384]{0:T(512)}) all-reduce(f32[384]{0:T(512)S(1)} %get-tuple-element.20, f32[384]{0:T(512)S(1)} %convert_reduce_fusion), channel_id=1, replica_groups=mesh['gx'=4,'gy'=4,'gz'=16] {'gy'}, use_global_device_ids=true, to_apply=%region_6.0 | all-reduce | flops 768 | bytes 6144 | tf_op jit(solution)/shard_map/psum | solution.py:75
  446.5 16.5 %reduce-scatter.11.cloned.1.call-done = bf16[64,384]{1,0:T(8,128)(2,1)} async-done(((bf16[256,384]{1,0:T(8,128)(2,1)}), bf16[64,384]{1,0:T(8,128)(2,1)}) %reduce-scatter.11.cloned.1.call-update) | async-done | bytes 49168 | tf_op jit(solution)/shard_map/reduce_scatter | solution.py:47
  463.0 1.4 add_convert_fusion
  464.5 54.5 %reduce-scatter.15.cloned.1.call-done = bf16[384,1536]{0,1:T(8,128)(2,1)} async-done(((bf16[384,6144]{0,1:T(8,128)(2,1)}), bf16[384,1536]{0,1:T(8,128)(2,1)}) %reduce-scatter.15.cloned.1.call-update) | async-done | bytes 1179664 | tf_op jit(solution)/shard_map/reduce_scatter | solution.py:70
  519.0 2.4 copy.13
  521.3 32.2 %reduce-scatter.13.cloned.1.call-done = bf16[64,384]{1,0:T(8,128)(2,1)} async-done(((bf16[256,384]{1,0:T(8,128)(2,1)}), bf16[64,384]{1,0:T(8,128)(2,1)}) %reduce-scatter.13.cloned.1.call-update) | async-done | bytes 49168 | tf_op jit(solution)/shard_map/reduce_scatter | solution.py:66
  553.6 56.4 %reduce-scatter.17.cloned.1.call-done = bf16[1536,384]{1,0:T(8,128)(2,1)} async-done(((bf16[6144,384]{1,0:T(8,128)(2,1)}), bf16[1536,384]{1,0:T(8,128)(2,1)}) %reduce-scatter.17.cloned.1.call-update) | async-done | bytes 1179664 | tf_op jit(solution)/shard_map/reduce_scatter | solution.py:62
  (23 shorter events, 0.5 us)
Async XLA Ops:
  7.2 61.6 %all-gather.5.cloned.1.call-start = ((), (), s32[]{:S(2)}) async-start(), calls=%async_computation.6 | async-start | bytes 5898240 | tf_op jit(solution)/shard_map/all_gather | solution.py:36
  7.9 118.4 %all-gather.9.cloned.1.call-start = ((), (), s32[]{:S(2)}) async-start(), calls=%async_computation.8 | async-start | bytes 5898240 | tf_op jit(solution)/shard_map/all_gather | solution.py:38
  8.6 188.2 %reduce-scatter.19.cloned.1.call-start = ((), (), s32[]{:S(2)}) async-start(), calls=%async_computation.14 | async-start | bytes 3342336
  75.8 0.8 copy-start.1
  75.8 198.0 %reduce-scatter.21.cloned.1.call-start = ((), (), s32[]{:S(2)}) async-start(), calls=%async_computation.15 | async-start | bytes 3342336
  133.3 141.6 %copy-start.2 = (f32[384]{0:T(512)S(1)}, f32[384]{0:T(512)}, u32[]{:S(2)}) copy-start(f32[384]{0:T(512)} %param.8) | copy-start | bytes 4612
  133.4 213.8 %all-gather.7.cloned.1.call-start = ((), (), s32[]{:S(2)}) async-start(), calls=%async_computation.7 | async-start | bytes 3342336 | tf_op jit(solution)/shard_map/all_gather | solution.py:45
  276.0 145.4 %all-gather.11.cloned.1.call-start = ((), (), s32[]{:S(2)}) async-start(), calls=%async_computation.10 | async-start | bytes 3342336 | tf_op jit(solution)/shard_map/all_gather | solution.py:60
  276.6 186.4 %reduce-scatter.11.cloned.1.call-start = ((), (), s32[]{:S(2)}) async-start(), calls=%async_computation.9 | async-start | bytes 245760 | tf_op jit(solution)/shard_map/reduce_scatter | solution.py:47
  352.9 166.1 %reduce-scatter.15.cloned.1.call-start = ((), (), s32[]{:S(2)}) async-start(), calls=%async_computation.12 | async-start | bytes 5898240 | tf_op jit(solution)/shard_map/reduce_scatter | solution.py:70
  427.4 6.1 copy-start
  427.4 126.2 %reduce-scatter.13.cloned.1.call-start = ((), (), s32[]{:S(2)}) async-start(), calls=%async_computation.11 | async-start | bytes 245760 | tf_op jit(solution)/shard_map/reduce_scatter | solution.py:66
  433.4 176.6 %reduce-scatter.17.cloned.1.call-start = ((), (), s32[]{:S(2)}) async-start(), calls=%async_computation.13 | async-start | bytes 5898240 | tf_op jit(solution)/shard_map/reduce_scatter | solution.py:62
  437.4 25.6 %copy-start.3 = (f32[384]{0:T(512)S(1)}, f32[384]{0:T(512)}, u32[]{:S(2)}) copy-start(f32[384]{0:T(512)} %param.10) | copy-start | bytes 4612
Sparse Core Ops, SparseCore 0:
  9.8 58.9 all-gather.4
  70.6 55.6 all-gather.8
  128.9 67.9 reduce-scatter.18
  199.3 74.5 reduce-scatter.20
  276.2 70.9 all-gather.6
  349.4 72.0 all-gather.10
  424.7 38.2 reduce-scatter.10
  465.6 53.3 reduce-scatter.14
  522.2 31.2 reduce-scatter.12
  556.6 53.3 reduce-scatter.16
where the time goes:
time: 617 us
  waiting for transfers between devices  532 us (86%)
  matrix products  29.9 us (5%)
  blocking collectives  27.1 us (4%)
  between operations  14.2 us (2%)
  local copies, waits for them, and re-layouts  11 us (2%)
    unnamed x12, waiting for transfers between devices  141 us
    all_gather x1, waiting for transfers between devices, per_device(): lax.all_gather(gelu_value(pre_act).astype(jnp.bfloat16), 'gz', axis=1, ti...  70.5 us
    all_gather x1, waiting for transfers between devices, per_device(): grad_full = lax.all_gather(grad_own, 'gz', axis=1, tiled=True)  68.5 us
    reduce_scatter x1, waiting for transfers between devices, per_device(): lax.psum_scatter(contract_rows(portion, cot_rows).astype(jnp.bfloat16), '...  56.4 us
    reduce_scatter x1, waiting for transfers between devices, per_device(): lax.psum_scatter(up_partial.astype(jnp.bfloat16), 'gy', scatter_dimension...  54.5 us
    all_gather x1, waiting for transfers between devices, per_device(): up_block = lax.all_gather(w_up, 'gy', axis=1, tiled=True)  49.7 us
    all_gather x1, waiting for transfers between devices, per_device(): down_block = lax.all_gather(w_down, 'gy', axis=0, tiled=True)  42.1 us
    reduce_scatter x1, waiting for transfers between devices, per_device(): lax.psum_scatter(contract_cols(portion, up_block).astype(jnp.bfloat16), '...  32.2 us
  transfers between devices with their start and end apart: 10, of which 10 were waited for; matrix products, arithmetic and copies ran while one was open for 7% of the time, Pallas kernels for 0%

commit v1 on v0

v1 whole, which is shorter than its diff:
```python
import jax
import jax.numpy as jnp
from jax import lax
from jax.sharding import PartitionSpec as P

gelu_scale = 0.7978845608028654
gelu_cubic = 0.044715


def gelu_both(v):
    t = jnp.tanh(gelu_scale * (v + gelu_cubic * v * v * v))
    value = 0.5 * v * (1.0 + t)
    slope = 0.5 * (1.0 + t) + 0.5 * v * (1.0 - t * t) * gelu_scale * (
        1.0 + 3.0 * gelu_cubic * v * v
    )
    return value, slope


def contract_rows(left, right):
    return lax.dot_general(
        left, right, (((0,), (0,)), ((), ())), preferred_element_type=jnp.float32
    )


def contract_cols(left, right):
    return lax.dot_general(
        left, right, (((1,), (1,)), ((), ())), preferred_element_type=jnp.float32
    )


def per_device(tokens, w_up, b_up, w_down, b_down, cotangent):
    rows_axes = ("gx", "gy")
    tok, cot = lax.all_gather((tokens, cotangent), rows_axes, axis=0, tiled=True)
    width = w_up.shape[1]
    small = b_up.shape[0]
    bias = lax.all_gather(b_up, "gz", axis=0, tiled=True)
    bias = lax.dynamic_slice_in_dim(bias, lax.axis_index("gy") * width, width, 0)

    partial_pre = jnp.dot(tok, w_up, preferred_element_type=jnp.float32).astype(jnp.bfloat16)
    partial_grad = contract_cols(cot, w_down).astype(jnp.bfloat16)
    pre = lax.psum_scatter(partial_pre, "gz", scatter_dimension=0, tiled=True)
    grad_act = lax.psum_scatter(partial_grad, "gz", scatter_dimension=0, tiled=True)
    value, slope = gelu_both(pre.astype(jnp.float32) + bias[None, :])
    act = lax.all_gather(value.astype(jnp.bfloat16), "gz", axis=0, tiled=True)
    grad_own = (grad_act.astype(jnp.float32) * slope).astype(jnp.bfloat16)
    grad = lax.all_gather(grad_own, "gz", axis=0, tiled=True)

    out = lax.psum_scatter(
        jnp.dot(act, w_down, preferred_element_type=jnp.float32).astype(jnp.bfloat16),
        rows_axes, scatter_dimension=0, tiled=True,
    )
    output = (out.astype(jnp.float32) + b_down[None, :]).astype(jnp.bfloat16)
    grad_w_down = contract_rows(act, cot).astype(jnp.bfloat16)
    grad_tokens = lax.psum_scatter(
        contract_cols(grad, w_up).astype(jnp.bfloat16), rows_axes, scatter_dimension=0, tiled=True
    )
    grad_w_up = contract_rows(tok, grad).astype(jnp.bfloat16)
    bias_sum = lax.all_gather(jnp.sum(grad.astype(jnp.float32), axis=0), "gy", axis=0, tiled=True)
    grad_b_up = lax.dynamic_slice_in_dim(bias_sum, lax.axis_index("gz") * small, small, 0)
    grad_b_down = jnp.sum(cot.astype(jnp.float32), axis=0)
    return (output, grad_tokens, grad_w_up, grad_b_up, grad_w_down, grad_b_down)


def solution(mesh):
    rows = P(("gx", "gy"), "gz")
    up = P("gz", ("gx", "gy"))
    down = P(("gx", "gy"), "gz")
    return jax.shard_map(
        per_device,
        mesh=mesh,
        in_specs=(rows, up, P(("gx", "gz")), down, P("gz"), rows),
        out_specs=(rows, rows, up, P(("gx", "gz")), down, P("gz")),
        check_vma=False,
    )
```

time: 617 us -> 514 us (0.83)
  waiting for transfers between devices: 532 us -> 347 us
  blocking collectives: 27.1 us -> 115 us
  local copies, waits for them, and re-layouts: 11 us -> 3.81 us
    unnamed x12 -> x6, waiting for transfers between devices: 141 us -> 0.6 us
    all_gather x2 -> x4, blocking collectives: 18 us -> 115 us  [the longest x2 75.7 us: per_device(): lax.all_gather((tokens, cotangent), rows_axes, axis=0, tiled=True)]
    all_gather x4 -> x2, waiting for transfers between devices: 231 us -> 141 us  [the longest x1 71.6 us: per_device(): act = lax.all_gather(value.astype(jnp.bfloat16), 'gz', axis=0, tiled=True)]
    reduce_scatter x4, waiting for transfers between devices: 160 us -> 206 us  [the longest x1 76.4 us: per_device(): lax.psum_scatter(contract_cols(grad, w_up).astype(jnp.bfloat16), rows_axe...]
    psum x1 -> x0, blocking collectives: 9.02 us -> none  [per_device(): grad_b_up, grad_b_down = lax.psum((bias_up_local, bias_down_local), 'gy')]
    unnamed x13 -> x17, local copies, waits for them, and re-layouts: 11 us -> 3.08 us
  transfers between devices with their start and end apart: 10 -> 6, of which waited for: 10 -> 5; matrix products, arithmetic and copies ran while one was open for 7% -> 5% of each run, Pallas kernels for 0% -> 0%
where the time goes in v1:
time: 514 us; the launch traced here: 513 us
  waiting for transfers between devices  347 us (68%)
  blocking collectives  115 us (22%)
  matrix products  25.4 us (5%)
  between operations  14.2 us (3%)
  other arithmetic  6.78 us (1%)
    reduce_scatter x1, waiting for transfers between devices, per_device(): lax.psum_scatter(contract_cols(grad, w_up).astype(jnp.bfloat16), rows_axe...  76.4 us
    all_gather x2, blocking collectives, per_device(): lax.all_gather((tokens, cotangent), rows_axes, axis=0, tiled=True)  75.7 us
    reduce_scatter x1, waiting for transfers between devices, per_device(): lax.psum_scatter(partial_grad, 'gz', scatter_dimension=0, tiled=True)  74.2 us
    all_gather x1, waiting for transfers between devices, per_device(): act = lax.all_gather(value.astype(jnp.bfloat16), 'gz', axis=0, tiled=True)  71.6 us
    all_gather x1, waiting for transfers between devices, per_device(): grad = lax.all_gather(grad_own, 'gz', axis=0, tiled=True)  69.1 us
    reduce_scatter x1, waiting for transfers between devices, per_device(): lax.psum_scatter(jnp.dot(act, w_down, preferred_element_type=jnp.float32)...  55.3 us
    all_gather x1, blocking collectives, per_device(): bias = lax.all_gather(b_up, 'gz', axis=0, tiled=True)  29.9 us
  transfers between devices with their start and end apart: 6, of which 5 were waited for; matrix products, arithmetic and copies ran while one was open for 5% of the time, Pallas kernels for 0%

profile of v1, /device:TPU:1, one launch (start us, length us, event | category | flops | bytes accessed | tf_op | source)
XLA Modules:
  0.0 512.6 jit_solution(12622350193706009672)
XLA Ops:
  7.2 0.0 reduce-scatter.5.cloned.1.call-start
  7.2 38.1 %all_gather.18 = bf16[1024,384]{1,0:T(8,128)(2,1)S(1)} all-gather(bf16[64,384]{1,0:T(8,128)(2,1)} %param.6), channel_id=1, replica_groups=mesh['gx'=4,'gy'=4,'gz'=16] {'gx','gy'}, dimensions={0}, use_global_device_ids=true | all-gather | bytes 835584 | tf_op jit(solution)/shard_map/all_gather | solution.py:33
  45.3 5.0 convolution_convert_fusion.1
  50.4 0.0 reduce-scatter.9.cloned.1.call-start
  50.4 0.7 copy-done.3
  51.1 37.6 %all_gather.21 = bf16[1024,384]{1,0:T(8,128)(2,1)S(1)} all-gather(bf16[64,384]{1,0:T(8,128)(2,1)S(1)} %copy-done.3), channel_id=1, replica_groups=mesh['gx'=4,'gy'=4,'gz'=16] {'gx','gy'}, dimensions={0}, use_global_device_ids=true | all-gather | bytes 835584 | tf_op jit(solution)/shard_map/all_gather | solution.py:33
  88.7 3.5 convolution_convert_fusion
  92.3 0.0 all-gather.5.cloned.1.call-start
  92.3 0.6 copy-done.5
  92.9 29.9 %all-gather = f32[16,1,384]{2,1,0:T(1,128)S(1)} all-gather(f32[1,1,384]{2,1,0:T(1,128)S(1)} %reshape.14), channel_id=1, replica_groups=mesh['gx'=4,'gy'=4,'gz'=16] {'gz'}, dimensions={0}, use_global_device_ids=true | all-gather | bytes 26112 | tf_op jit(solution)/shard_map/all_gather | solution.py:36
  122.8 0.1 dynamic_slice.6
  122.9 74.2 %reduce-scatter.9.cloned.1.call-done = bf16[64,1536]{1,0:T(8,128)(2,1)} async-done(((bf16[1024,1536]{1,0:T(8,128)(2,1)}), bf16[64,1536]{1,0:T(8,128)(2,1)}) %reduce-scatter.9.cloned.1.call-update) | async-done | bytes 196624 | tf_op jit(solution)/shard_map/reduce_scatter | solution.py:42
  197.1 2.1 fusion.7
  199.2 0.0 all-gather.7.cloned.1.call-start
  199.3 0.5 all-gather.7.cloned.1.call-update
  199.8 0.0 reduce-scatter.7.cloned.1.call-start
  199.8 71.6 %all-gather.5.cloned.1.call-done = bf16[1024,1536]{1,0:T(8,128)(2,1)} async-done(((bf16[64,1536]{1,0:T(8,128)(2,1)}), bf16[1024,1536]{1,0:T(8,128)(2,1)}) %all-gather.5.cloned.1.call-update) | async-done | bytes 3145744 | tf_op jit(solution)/shard_map/all_gather | solution.py:44
  271.4 4.6 convolution_convert_fusion.5
  276.0 0.0 reduce-scatter.11.cloned.1.call-start
  276.1 0.7 convert_reduce_fusion.1
  276.8 69.1 %all-gather.7.cloned.1.call-done = bf16[1024,1536]{1,0:T(8,128)(2,1)} async-done(((bf16[64,1536]{1,0:T(8,128)(2,1)}), bf16[1024,1536]{1,0:T(8,128)(2,1)}) %all-gather.7.cloned.1.call-update) | async-done | bytes 3145744 | tf_op jit(solution)/shard_map/all_gather | solution.py:46
  345.9 4.6 convolution_convert_fusion.4
  350.5 2.5 convert_reduce_fusion
  353.1 0.3 copy-done.1
  353.4 3.0 fusion
  356.3 1.5 copy.13
  357.8 9.4 %all-gather.1 = f32[4,1,1536]{2,1,0:T(1,128)S(1)} all-gather(f32[1,1,1536]{2,1,0:T(1,128)S(1)} %reshape.16), channel_id=1, replica_groups=mesh['gx'=4,'gy'=4,'gz'=16] {'gy'}, dimensions={0}, use_global_device_ids=true | all-gather | bytes 30720 | tf_op jit(solution)/shard_map/all_gather | solution.py:58
  367.1 0.7 dynamic_slice.7
  367.8 4.8 convolution_convert_fusion.2
  372.6 55.3 %reduce-scatter.7.cloned.1.call-done = bf16[64,384]{1,0:T(8,128)(2,1)} async-done(((bf16[1024,384]{1,0:T(8,128)(2,1)}), bf16[64,384]{1,0:T(8,128)(2,1)}) %reduce-scatter.7.cloned.1.call-update) | async-done | bytes 49168 | tf_op jit(solution)/shard_map/reduce_scatter | solution.py:48
  427.9 1.4 add_convert_fusion
  429.3 76.4 %reduce-scatter.11.cloned.1.call-done = bf16[64,384]{1,0:T(8,128)(2,1)} async-done(((bf16[1024,384]{1,0:T(8,128)(2,1)}), bf16[64,384]{1,0:T(8,128)(2,1)}) %reduce-scatter.11.cloned.1.call-update) | async-done | bytes 49168 | tf_op jit(solution)/shard_map/reduce_scatter | solution.py:54
  (19 shorter events, 0.1 us)
Async XLA Ops:
  7.2 81.6 %copy-start = (bf16[1536,384]{1,0:T(8,128)(2,1)S(1)}, bf16[1536,384]{1,0:T(8,128)(2,1)}, u32[]{:S(2)}) copy-start(bf16[1536,384]{1,0:T(8,128)(2,1)} %param.9) | copy-start | bytes 3538948
  7.2 115.7 %reduce-scatter.5.cloned.1.call-start = ((), (), s32[]{:S(2)}) async-start(), calls=%async_computation.4 | async-start | bytes 3342336 | tf_op jit(solution)/shard_map/reduce_scatter | solution.py:41
  45.3 5.0 copy-start.2
  50.3 0.8 copy-start.3
  50.4 146.8 %reduce-scatter.9.cloned.1.call-start = ((), (), s32[]{:S(2)}) async-start(), calls=%async_computation.7 | async-start | bytes 3342336 | tf_op jit(solution)/shard_map/reduce_scatter | solution.py:42
  92.2 0.7 copy-start.5
  92.3 179.2 %all-gather.5.cloned.1.call-start = ((), (), s32[]{:S(2)}) async-start(), calls=%async_computation.5 | async-start | bytes 3342336 | tf_op jit(solution)/shard_map/all_gather | solution.py:44
  199.2 146.7 %all-gather.7.cloned.1.call-start = ((), (), s32[]{:S(2)}) async-start(), calls=%async_computation.8 | async-start | bytes 3342336 | tf_op jit(solution)/shard_map/all_gather | solution.py:46
  199.8 146.1 %copy-start.6 = (bf16[384,1536]{1,0:T(8,128)(2,1)S(1)}, bf16[384,1536]{1,0:T(8,128)(2,1)}, u32[]{:S(2)}) copy-start(bf16[384,1536]{1,0:T(8,128)(2,1)} %param.7) | copy-start | bytes 3538948
  199.8 228.1 %reduce-scatter.7.cloned.1.call-start = ((), (), s32[]{:S(2)}) async-start(), calls=%async_computation.6 | async-start | bytes 835584 | tf_op jit(solution)/shard_map/reduce_scatter | solution.py:48
  276.0 229.7 %reduce-scatter.11.cloned.1.call-start = ((), (), s32[]{:S(2)}) async-start(), calls=%async_computation.9 | async-start | bytes 835584 | tf_op jit(solution)/shard_map/reduce_scatter | solution.py:54
  350.5 2.8 copy-start.1
  367.8 60.1 %copy-start.4 = (f32[384]{0:T(512)S(1)}, f32[384]{0:T(512)}, u32[]{:S(2)}) copy-start(f32[384]{0:T(512)} %param.10) | copy-start | bytes 4612
Sparse Core Ops, SparseCore 0:
  50.5 71.1 reduce-scatter.4
  124.3 72.8 reduce-scatter.8
  199.3 72.0 all-gather.4
  273.7 72.2 all-gather.6
  349.9 77.9 reduce-scatter.6
  433.0 72.7 reduce-scatter.10

commit v2 on v1

v2 whole, which is shorter than its diff:
```python
import functools

import jax
import jax.numpy as jnp
from jax import lax
from jax.experimental import pallas as pl
from jax.experimental.pallas import tpu as pltpu
from jax.sharding import PartitionSpec as P

BF = jnp.bfloat16
F32 = jnp.float32
MESH = pl.DeviceIdType.MESH
gelu_scale = 0.7978845608028654
gelu_cubic = 0.044715
NC = 4
NZ = 8
TILE = 512
RS_GRAD, RS_PRE, AG_ACT, AG_GRAD = 0, 1, 2, 3
X_PRE, X_GRAD, X_AG, X_ACT = 0, 1, 2, 3


def gelu_both(v):
    t = jnp.tanh(gelu_scale * (v + gelu_cubic * v * v * v))
    value = 0.5 * v * (1.0 + t)
    slope = 0.5 * (1.0 + t) + 0.5 * v * (1.0 - t * t) * gelu_scale * (
        1.0 + 3.0 * gelu_cubic * v * v
    )
    return value, slope


def dot_nt(left, right):
    return lax.dot_general(left, right, (((1,), (1,)), ((), ())), preferred_element_type=F32)


def kernel(
    tok_ref, wup_ref, bup_ref, wdn_ref, bdn_ref, cot_ref,
    out_ref, gtok_ref, gwu_ref, gbu_ref, gwd_ref, gbd_ref,
    tc, tct, ppre, pgrad, xpre, zpre, zgrad, xgrad, act, grad, gact, acc_u, acc_d,
    opart, rcore, sx, rx, sy, ry, cs, bs, ball, brow,
    zs, zr, xs, xr, hs, hr, fs, fr, bzs, bzr,
):
    gx, gy, gz = lax.axis_index("gx"), lax.axis_index("gy"), lax.axis_index("gz")
    z, xl = lax.rem(gz, NZ), lax.div(gz, NZ)
    xo = 1 - xl
    xh, core = lax.div(gx, 2), lax.rem(gx, 2)
    feat, width = wup_ref.shape
    half = width // 2
    rows = tok_ref.shape[0]
    crow = 4 * rows
    unit = crow // 16

    def zi(j):
        return lax.rem(z + j + NZ, NZ)

    zdev = ({"gz": xl * NZ + zi(1)}, {"gz": xl * NZ + zi(-1)})
    xdev = {"gz": xo * NZ + z}
    coredev = {"gx": xh * 2 + 1 - core}
    xhdev = {"gx": (1 - xh) * 2 + core}

    def ydev(d):
        return {"gy": lax.rem(gy + d + 4, 4)}

    sign = (1, -1)

    def rcopy(src, dst, ss, rs, dev):
        return pltpu.make_async_remote_copy(
            src_ref=src, dst_ref=dst, send_sem=ss, recv_sem=rs,
            device_id=dev, device_id_type=MESH,
        )

    def hcols(ref, d):
        cols = pl.ds(d * half, half)
        return ref.at[..., cols] if not isinstance(ref, tuple) else None

    def rs_unit(op, u, t):
        return pgrad.at[u, t] if op == RS_GRAD else ppre.at[u, t, xl]

    def rs_land(op, u, d, r):
        return (zgrad if op == RS_GRAD else zpre).at[u, d, r - 1]

    def rs_copy(op, u, r, d):
        src = rs_unit(op, u, zi(sign[d] * (5 - r)))
        dst = rs_land(op, u, d, r)
        if r == 1:
            src, dst = hcols(src, d), hcols(dst, d)
        k = op * 8 + d * 4 + r - 1
        return rcopy(src, dst, zs.at[u, k], zr.at[u, k], zdev[d])

    def rs_step(op, u, r):
        for d in range(2):
            rs_copy(op, u, r - 1, d).wait_recv()
            dst, got = rs_unit(op, u, zi(sign[d] * (5 - r))), rs_land(op, u, d, r - 1)
            if r == 2:
                dst, got = hcols(dst, d), hcols(got, d)
            dst[...] = (dst[...].astype(F32) + got[...].astype(F32)).astype(BF)
            rs_copy(op, u, r, d).start()

    def ag_unit(op, u, t):
        return grad.at[u, t] if op == AG_GRAD else act.at[u, t, xl]

    def ag_copy(op, u, r, d, arriving):
        t = zi(-sign[d] * (r if arriving else r - 1))
        ref = ag_unit(op, u, t)
        if r == 4:
            ref = hcols(ref, d)
        k = op * 8 + d * 4 + r - 1
        return rcopy(ref, ref, zs.at[u, k], zr.at[u, k], zdev[d])

    def act_x(u, j, arriving):
        ref = act.at[u, zi(j), xo if arriving else xl]
        return rcopy(ref, ref, xs.at[u, X_ACT + j], xr.at[u, X_ACT + j], xdev)

    def ag_step(op, u, r):
        for d in range(2):
            ag_copy(op, u, r - 1, d, True).wait_recv()
            ag_copy(op, u, r, d, False).start()
            if op == AG_ACT:
                act_x(u, (-sign[d] * (r - 1)) % NZ, False).start()

    def x_pre(u):
        return rcopy(ppre.at[u, :, xo], xpre.at[u], xs.at[u, X_PRE], xr.at[u, X_PRE], xdev)

    def x_grad(u):
        return rcopy(pgrad.at[u, z, xo], xgrad.at[u], xs.at[u, X_GRAD], xr.at[u, X_GRAD], xdev)

    def x_ag(u, arriving):
        ref = grad.at[u, z, xo if arriving else xl]
        return rcopy(ref, ref, xs.at[u, X_AG], xr.at[u, X_AG], xdev)

    def bias_x(arriving):
        ref = ball.at[z, xo if arriving else xl]
        return rcopy(ref, ref, bzs.at[0], bzr.at[0], xdev)

    def bias_copy(r, d, arriving):
        ref = ball.at[zi(-sign[d] * (r if arriving else r - 1))]
        k = d * 4 + r
        return rcopy(ref, ref, bzs.at[k], bzr.at[k], zdev[d])

    def h_copy(k, src, dst, dev):
        return rcopy(src, dst, hs.at[k], hr.at[k], dev)

    own = tc.at[:, 0, xh, core]
    from_xh = tc.at[:, 0, 1 - xh, core]

    def h_xh():
        return h_copy(0, own, own, xhdev)

    def h_core():
        return h_copy(1, own, own, coredev)

    def h_core_fwd():
        return h_copy(2, from_xh, from_xh, coredev)

    def h_y(d):
        return h_copy(2 + d, own, tc.at[:, d, xh, core], ydev(-d))

    def h_y_fwd(d):
        return h_copy(5 + d, from_xh, tc.at[:, d, 1 - xh, core], ydev(-d))

    def h_core_y(d):
        ref = tc.at[:, d, :, core]
        return h_copy(8 + d, ref, ref, coredev)

    def part_pre(u):
        x = tc[0, u].reshape(crow, feat)

        @pl.loop(0, width // TILE)
        def _(j):
            cols = pl.ds(pl.multiple_of(j * TILE, TILE), TILE)
            v = jnp.dot(x, wup_ref[:, cols], preferred_element_type=F32)
            ppre[u, :, :, :, cols] = v.astype(BF).reshape(NZ, 2, unit, TILE)

    def part_grad(u):
        x = tc[1, u].reshape(crow, feat)

        @pl.loop(0, width // TILE)
        def _(j):
            cols = pl.ds(pl.multiple_of(j * TILE, TILE), TILE)
            v = dot_nt(x, wdn_ref[cols, :])
            pgrad[u, :, :, :, cols] = v.astype(BF).reshape(NZ, 2, unit, TILE)

    def transposed(u):
        tct[0, u] = tc[0, u].reshape(crow, feat).T
        tct[1, u] = tc[1, u].reshape(crow, feat).T

    def gelu_unit(u):
        v = (
            ppre[u, z, xl].astype(F32) + zpre[u, 0, 3].astype(F32) + zpre[u, 1, 3].astype(F32)
        ) + brow[0:1, :]
        value, slope = gelu_both(v)
        act[u, z, xl] = value.astype(BF)
        g = gact[u] + xgrad[u].astype(F32)
        grad[u, z, xl] = (g * slope).astype(BF)

    def f_core(u):
        return rcopy(opart.at[u, :, :, 1 - core], rcore.at[u], fs.at[u, 0], fr.at[u, 0], coredev)

    def f_xh(u):
        return rcopy(sx.at[u], rx.at[u], fs.at[u, 1], fr.at[u, 1], xhdev)

    def f_y(u):
        return rcopy(sy.at[u], ry.at[u], fs.at[u, 2], fr.at[u, 2], ydev(u))

    def final_1(u):
        for j in range(NZ):
            act_x(u, j, True).wait_recv()
        o = jnp.dot(act[u].reshape(crow, width), wdn_ref[...], preferred_element_type=F32)
        opart[u, 0] = o.astype(BF).reshape(2, 2, rows, feat)
        o = dot_nt(grad[u].reshape(crow, width), wup_ref[...])
        opart[u, 1] = o.astype(BF).reshape(2, 2, rows, feat)
        f_core(u).start()

    def weight_grad(acc, side, full, u):
        @pl.loop(0, width // TILE)
        def _(j):
            cols = pl.ds(pl.multiple_of(j * TILE, TILE), TILE)
            acc[:, cols] += jnp.dot(
                tct[side, u], full[u, :, :, :, cols].reshape(crow, TILE),
                preferred_element_type=F32,
            )

    def final_2(u):
        f_core(u).wait_recv()
        mine = opart[u, :, 1 - xh, core].astype(F32) + rcore[u, :, 1 - xh].astype(F32)
        sx[u] = mine.astype(BF)
        f_xh(u).start()

    def final_3(u):
        f_xh(u).wait_recv()
        mine = (
            opart[u, :, xh, core].astype(F32) + rcore[u, :, xh].astype(F32) + rx[u].astype(F32)
        ).astype(BF)

        @pl.when(u == 0)
        def _():
            ry[0] = mine

        @pl.when(u > 0)
        def _():
            sy[u] = mine
            f_y(u).start()

    def col_sum(u):
        cs[...] += jnp.sum(grad[u].reshape(crow // 8, 8, width).astype(F32), axis=0)

    for side, ref in ((0, tok_ref), (1, cot_ref)):
        tc[side, 0, xh, core] = ref[...]
    ball[z, xl] = jnp.broadcast_to(bup_ref[...], ball.shape[2:])
    acc_u[...] = jnp.zeros_like(acc_u)
    acc_d[...] = jnp.zeros_like(acc_d)
    cs[...] = jnp.zeros_like(cs)

    barrier = pltpu.get_barrier_semaphore()
    peers = (zdev[0], zdev[1], xdev, coredev, xhdev, ydev(1), ydev(2), ydev(3))
    for dev in peers:
        pl.semaphore_signal(barrier, inc=1, device_id=dev, device_id_type=MESH)
    pl.semaphore_wait(barrier, len(peers))

    h_xh().start()
    h_core().start()
    for d in (1, 2, 3):
        h_y(d).start()
    bias_x(False).start()
    h_xh().wait_recv()
    h_core_fwd().start()
    for d in (1, 2, 3):
        h_y_fwd(d).start()
    h_core().wait_recv()
    h_core_fwd().wait_recv()
    part_grad(0)
    part_pre(0)
    for d in (1, 2, 3):
        h_y(d).wait_recv()
        h_y_fwd(d).wait_recv()
        h_core_y(d).start()
    transposed(0)

    def slot(s, carry):
        ug, up, ua, uf = s, s - 1, s - 2, s - 3
        on_g = s <= 3
        on_p = (s >= 1) & (s <= 4)
        on_a = (s >= 2) & (s <= 5)
        on_f = s >= 3

        @pl.when(on_g)
        def _():
            x_pre(ug).start()
            for d in range(2):
                rs_copy(RS_GRAD, ug, 1, d).start()

        @pl.when(on_p)
        def _():
            x_pre(up).wait_recv()
            ppre[up, :, xl] = (ppre[up, :, xl].astype(F32) + xpre[up].astype(F32)).astype(BF)
            for d in range(2):
                rs_copy(RS_PRE, up, 1, d).start()

        @pl.when(on_a)
        def _():
            x_ag(ua, True).wait_recv()
            for d in range(2):
                ag_copy(AG_GRAD, ua, 1, d, False).start()

        @pl.when(s == 0)
        def _():
            bias_x(True).wait_recv()
            for d in range(2):
                bias_copy(1, d, False).start()

        for r in (2, 3, 4):
            @pl.when(on_g)
            def _():
                rs_step(RS_GRAD, ug, r)

            @pl.when(on_p)
            def _():
                rs_step(RS_PRE, up, r)

            @pl.when(on_a)
            def _():
                ag_step(AG_ACT, ua, r)
                ag_step(AG_GRAD, ua, r)

            @pl.when(s == 0)
            def _():
                for d in range(2):
                    bias_copy(r - 1, d, True).wait_recv()
                    if r < 4 or d == 0:
                        bias_copy(r, d, False).start()

            if r == 2:
                @pl.when(s < 3)
                def _():
                    un = s + 1
                    h_wait = rcopy(
                        tc.at[:, un, :, 1 - core], tc.at[:, un, :, 1 - core],
                        hs.at[8 + un], hr.at[8 + un], coredev,
                    )
                    h_wait.wait_recv()
                    part_grad(un)

                @pl.when(on_f)
                def _():
                    final_1(uf)

            if r == 3:
                @pl.when(s < 3)
                def _():
                    part_pre(s + 1)
                    transposed(s + 1)

                @pl.when(on_f)
                def _():
                    weight_grad(acc_u, 0, grad, uf)
                    final_2(uf)

            if r == 4:
                @pl.when(on_f)
                def _():
                    weight_grad(acc_d, 1, act, uf)
                    col_sum(uf)
                    final_3(uf)

        @pl.when(on_a)
        def _():
            for d in range(2):
                ag_copy(AG_ACT, ua, 4, d, True).wait_recv()
            act_x(ua, 4, False).start()
            for d in range(2):
                ag_copy(AG_GRAD, ua, 4, d, True).wait_recv()

        @pl.when(on_g)
        def _():
            for d in range(2):
                rs_copy(RS_GRAD, ug, 4, d).wait_recv()

            def total(side):
                return (
                    pgrad[ug, z, side].astype(F32)
                    + zgrad[ug, 0, 3, side].astype(F32)
                    + zgrad[ug, 1, 3, side].astype(F32)
                )

            pgrad[ug, z, xo] = total(xo).astype(BF)
            x_grad(ug).start()
            gact[ug] = total(xl)

        @pl.when(s == 0)
        def _():
            bias_copy(4, 0, True).wait_recv()
            for j in range(4):
                piece = gy * 4 + j
                brow[:, j * feat:(j + 1) * feat] = ball[lax.rem(piece, NZ), lax.div(piece, NZ)]

        @pl.when(on_p)
        def _():
            for d in range(2):
                rs_copy(RS_PRE, up, 4, d).wait_recv()
            x_grad(up).wait_recv()
            gelu_unit(up)
            x_ag(up, False).start()
            for d in range(2):
                ag_copy(AG_ACT, up, 1, d, False).start()
            act_x(up, 0, False).start()

        return carry

    lax.fori_loop(0, NC + 3, slot, 0)

    piece = pl.ds(pl.multiple_of(lax.rem(gz, 4) * feat, 128), feat)
    bs[gy] = cs[:, piece]

    def b_y(d):
        return rcopy(bs.at[gy], bs.at[gy], hs.at[11 + d], hr.at[11 + d], ydev(d))

    for d in (1, 2, 3):
        b_y(d).start()

    gwu_ref[...] = acc_u[...].astype(BF)
    gwd_ref[...] = acc_d[...].astype(BF).T
    gbd_ref[...] = jnp.sum(
        tc[1].reshape(NC * crow, feat).astype(F32), axis=0, keepdims=True
    )
    for d in (1, 2, 3):
        src = lax.rem(gy - d + 4, 4)
        rcopy(bs.at[src], bs.at[src], hs.at[11 + d], hr.at[11 + d], ydev(d)).wait_recv()
    gbu_ref[...] = jnp.sum(bs[lax.div(gz, 4)], axis=0, keepdims=True)
    for d in (1, 2, 3):
        f_y(d).wait_recv()
    total = (ry[0].astype(F32) + ry[1].astype(F32)) + (ry[2].astype(F32) + ry[3].astype(F32))
    out_ref[...] = (total[0] + bdn_ref[...]).astype(BF)
    gtok_ref[...] = total[1].astype(BF)

    def drain(u, carry):
        for d in range(2):
            for r in range(1, 5):
                rs_copy(RS_GRAD, u, r, d).wait_send()
                rs_copy(RS_PRE, u, r, d).wait_send()
                ag_copy(AG_ACT, u, r, d, False).wait_send()
                ag_copy(AG_GRAD, u, r, d, False).wait_send()
        x_pre(u).wait_send()
        x_grad(u).wait_send()
        x_ag(u, False).wait_send()
        for j in range(NZ):
            act_x(u, j, False).wait_send()
        f_core(u).wait_send()
        f_xh(u).wait_send()

        @pl.when(u > 0)
        def _():
            f_y(u).wait_send()
        return carry

    lax.fori_loop(0, NC, drain, 0)
    h_xh().wait_send()
    h_core().wait_send()
    h_core_fwd().wait_send()
    for d in (1, 2, 3):
        h_y(d).wait_send()
        h_y_fwd(d).wait_send()
        h_core_y(d).wait_send()
        b_y(d).wait_send()
    bias_x(False).wait_send()
    for r in range(1, 5):
        for d in range(2):
            if r < 4 or d == 0:
                bias_copy(r, d, False).wait_send()


def per_device(tokens, w_up, b_up, w_down, b_down, cotangent):
    rows, feat = tokens.shape
    width = w_up.shape[1]
    crow = 4 * rows
    unit = crow // 16
    vmem = pl.BlockSpec(memory_space=pltpu.VMEM)
    full = (NC, NZ, 2, unit, width)
    dma = pltpu.SemaphoreType.DMA
    scratch = [
        pltpu.VMEM((2, NC, 2, 2, rows, feat), BF),
        pltpu.VMEM((2, NC, feat, crow), BF),
        pltpu.VMEM(full, BF),
        pltpu.VMEM(full, BF),
        pltpu.VMEM((NC, NZ, unit, width), BF),
        pltpu.VMEM((NC, 2, 4, unit, width), BF),
        pltpu.VMEM((NC, 2, 4, 2, unit, width), BF),
        pltpu.VMEM((NC, unit, width), BF),
        pltpu.VMEM(full, BF),
        pltpu.VMEM(full, BF),
        pltpu.VMEM((NC, unit, width), F32),
        pltpu.VMEM((feat, width), F32),
        pltpu.VMEM((feat, width), F32),
        pltpu.VMEM((NC, 2, 2, 2, rows, feat), BF),
        pltpu.VMEM((NC, 2, 2, rows, feat), BF),
        pltpu.VMEM((NC, 2, rows, feat), BF),
        pltpu.VMEM((NC, 2, rows, feat), BF),
        pltpu.VMEM((NC, 2, rows, feat), BF),
        pltpu.VMEM((NC, 2, rows, feat), BF),
        pltpu.VMEM((8, width), F32),
        pltpu.VMEM((4, 8, feat), F32),
        pltpu.VMEM((NZ, 2, 8, feat), F32),
        pltpu.VMEM((8, width), F32),
        dma((NC, 32)), dma((NC, 32)),
        dma((NC, 11)), dma((NC, 11)),
        dma((15,)), dma((15,)),
        dma((NC, 3)), dma((NC, 3)),
        dma((9,)), dma((9,)),
    ]
    out, gtok, gwu, gbu, gwd, gbd = pl.pallas_call(
        kernel,
        out_shape=(
            jax.ShapeDtypeStruct((rows, feat), BF),
            jax.ShapeDtypeStruct((rows, feat), BF),
            jax.ShapeDtypeStruct((feat, width), BF),
            jax.ShapeDtypeStruct((1, feat), F32),
            jax.ShapeDtypeStruct((width, feat), BF),
            jax.ShapeDtypeStruct((1, feat), F32),
        ),
        in_specs=[vmem] * 6,
        out_specs=(vmem,) * 6,
        scratch_shapes=scratch,
        compiler_params=pltpu.CompilerParams(
            collective_id=0, has_side_effects=True, vmem_limit_bytes=60 * 2**20
        ),
        name="mlp_block",
    )(tokens, w_up, b_up[None, :], w_down, b_down[None, :], cotangent)
    return out, gtok, gwu, gbu[0], gwd, gbd[0]


def solution(mesh):
    rows = P(("gx", "gy"), "gz")
    up = P("gz", ("gx", "gy"))
    down = P(("gx", "gy"), "gz")
    return jax.shard_map(
        per_device,
        mesh=mesh,
        in_specs=(rows, up, P(("gx", "gz")), down, P("gz"), rows),
        out_specs=(rows, rows, up, P(("gx", "gz")), down, P("gz")),
        check_vma=False,
    )
```

time: 514 us -> 175 us (0.34)
  waiting for transfers between devices: 347 us -> 0 us
  Pallas kernels: 0 us -> 163 us
  blocking collectives: 115 us -> 0 us
  matrix products: 25.4 us -> 0 us
  between operations: 14.2 us -> 0.64 us
    reduce_scatter x4 -> x0, waiting for transfers between devices: 206 us -> none  [the longest x1 76.4 us: per_device(): lax.psum_scatter(contract_cols(grad, w_up).astype(jnp.bfloat16), rows_axe...]
    pallas_call x0 -> x1, Pallas kernels: none -> 163 us  [per_device(): pl.pallas_call(kernel, out_shape=(jax.ShapeDtypeStruct((rows, feat), BF),...]
    all_gather x2 -> x0, waiting for transfers between devices: 141 us -> none  [the longest x1 71.6 us: per_device(): act = lax.all_gather(value.astype(jnp.bfloat16), 'gz', axis=0, tiled=True)]
    all_gather x4 -> x0, blocking collectives: 115 us -> none  [the longest x2 75.7 us: per_device(): lax.all_gather((tokens, cotangent), rows_axes, axis=0, tiled=True)]
    dot_general x6 -> x0, matrix products: 25.4 us -> none  [the longest x2 8.09 us: contract_cols(): lax.dot_general(left, right, (((1,), (1,)), ((), ())), preferred_element_...]
  transfers between devices with their start and end apart: 6 -> 0, of which waited for: 5 -> 0; matrix products, arithmetic and copies ran while one was open for 5% -> 0% of each run, Pallas kernels for 0% -> 0%
where the time goes in v2:
time: 175 us; the launch traced here: 174 us
  Pallas kernels  163 us (93%)
  local copies, waits for them, and re-layouts  8.81 us (5%)
  other arithmetic  2.51 us (1%)
    pallas_call x1, Pallas kernels, per_device(): pl.pallas_call(kernel, out_shape=(jax.ShapeDtypeStruct((rows, feat), BF),...  163 us
    unnamed x6, local copies, waits for them, and re-layouts  6.32 us

profile of v2, /device:TPU:1, one launch (start us, length us, event | category | flops | bytes accessed | tf_op | source)
XLA Modules:
  0.0 174.5 jit_solution(3842209846946265199)
XLA Ops:
  0.6 1.2 broadcast_in_dim.6.bup_ref
  1.9 1.2 broadcast_in_dim.7.bdn_ref
  3.1 162.5 %mlp_block.1 = (bf16[64,384]{1,0:T(8,128)(2,1)}, bf16[64,384]{1,0:T(8,128)(2,1)}, bf16[384,1536]{1,0:T(8,128)(2,1)}, f32[1,384]{1,0:T(1,128)}, bf16[1536,384]{1,0:T(8,128)(2,1)}, /*index=5*/f32[1,384]{1,0:T(1,128)}) custom-call(bf16[64,384]{1,0:T(8,128)(2,1)} %tok_ref.1, bf16[384,1536]{1,0:T(8,128)(2,1)} %wup_ref.1, f32[1,384]{1,0:T(1,128)} %broadcast_in_dim.6.bup_ref, ...), custom_call_target="tpu_custom_call" | custom-call | tf_op jit(solution)/shard_map/mlp_block/pallas_call | solution.py:508
  165.6 1.3 reduce
  166.9 1.2 reduce.1
  168.1 1.4 copy.16
  169.6 1.4 copy.17
  171.0 0.0 copy-start
  171.0 2.5 %copy.18 = bf16[384,1536]{1,0:T(8,128)(2,1)} copy(bf16[384,1536]{1,0:T(8,128)(2,1)} %get-tuple-element.26) | data formatting | bytes 2359296
  173.5 0.0 copy-done
  173.5 1.0 copy.19
Async XLA Ops:
  171.0 2.5 %copy-start = (bf16[1536,384]{1,0:T(8,128)(2,1)S(1)}, bf16[1536,384]{1,0:T(8,128)(2,1)}, u32[]{:S(2)}) copy-start(bf16[1536,384]{1,0:T(8,128)(2,1)} %get-tuple-element.28) | copy-start | bytes 3538948

commit v3 on v1

v3 whole, which is shorter than its diff:
```python
import jax
import jax.numpy as jnp
from jax import lax
from jax.experimental import pallas as pl
from jax.experimental.pallas import tpu as pltpu
from jax.sharding import PartitionSpec as P

BF = jnp.bfloat16
F32 = jnp.float32
MESH = pl.DeviceIdType.MESH
gelu_scale = 0.7978845608028654
gelu_cubic = 0.044715
NZ = 8
CHUNKS = ((0, 0), (1, 0), (1, 1), (2, 0), (2, 1), (3, 0), (3, 1), (0, 1))
NC = len(CHUNKS)
SIGN = (1, -1)
PRE, GRAD = 0, 1
LAG = 30

RS_X = ((1, 1, 0, 1, 1, 1, 0, 1), (0, 0, 1, 0, 1, 1, 0, 0))
AG_X = ((1, 1, 0, 1, 0, 1, 1, 1), (1, 0, 0, 1, 1, 0, 1, 0))
ORDER = (
    ("H", 0, 0), ("PP", 0, 1), ("PP", 0, 0), ("HF", 1, 0), ("HX", 0, 0), ("B1", 0, 0),
    ("R2", 0, 1), ("PP", 1, 1), ("HF", 3, 0), ("PP", 1, 0), ("B2", 0, 0), ("PP", 7, 1),
    ("R3", 0, 1), ("HF", 5, 0), ("PP", 3, 1), ("R1", 0, 0), ("B3", 0, 0), ("R2", 1, 1),
    ("R2", 7, 1), ("HF", 2, 0), ("PP", 3, 0), ("R4", 0, 1), ("R2", 3, 1), ("R2", 0, 0),
    ("HF", 4, 0), ("B4", 0, 0), ("PP", 2, 1), ("R1", 1, 0), ("R3", 1, 1), ("PP", 2, 0),
    ("HF", 6, 0), ("R3", 7, 1), ("PP", 4, 1), ("R5", 0, 1), ("PP", 4, 0), ("R3", 3, 1),
    ("R3", 0, 0), ("B5", 0, 0), ("R1", 3, 0), ("R2", 1, 0), ("PP", 5, 1), ("R4", 1, 1),
    ("R2", 2, 0), ("PP", 5, 0), ("R4", 7, 1), ("PP", 6, 1), ("R4", 3, 1), ("R4", 0, 0),
    ("R1", 2, 1), ("R3", 1, 0), ("R2", 3, 0), ("PP", 6, 0), ("R5", 1, 1), ("PP", 7, 0),
    ("R3", 2, 0), ("R1", 4, 1), ("R5", 7, 1), ("R2", 6, 1), ("D", 0, 0), ("R5", 3, 1),
    ("E", 0, 0), ("R4", 1, 0), ("R2", 2, 1), ("R3", 3, 0), ("R2", 6, 0), ("R1", 4, 0),
    ("R4", 2, 0), ("R2", 4, 1), ("R3", 6, 1), ("A2", 0, 0), ("A2", 0, 1), ("R3", 2, 1),
    ("R1", 5, 1), ("R4", 3, 0), ("R3", 6, 0), ("R2", 4, 0), ("R5", 2, 0), ("R3", 4, 1),
    ("R4", 6, 1), ("R1", 5, 0), ("A3", 0, 0), ("A3", 0, 1), ("E", 1, 0), ("R4", 2, 1),
    ("R2", 5, 1), ("R4", 6, 0), ("R3", 4, 0), ("R4", 4, 1), ("R1", 7, 0), ("R5", 6, 1),
    ("E", 3, 0), ("A4", 0, 0), ("A4", 0, 1), ("R2", 5, 0), ("A2", 1, 0), ("R3", 5, 1),
    ("R5", 6, 0), ("E", 2, 0), ("R4", 4, 0), ("R2", 7, 0), ("A2", 3, 0), ("A2", 3, 1),
    ("A5", 0, 0), ("A5", 0, 1), ("A1", 1, 1), ("R3", 5, 0), ("A3", 1, 0), ("R4", 5, 1),
    ("E", 4, 0), ("R3", 7, 0), ("A3", 3, 0), ("A3", 3, 1), ("A2", 1, 1), ("R4", 5, 0),
    ("E", 6, 0), ("A4", 1, 0), ("A1", 2, 0), ("A1", 2, 1), ("A2", 4, 1), ("R4", 7, 0),
    ("A4", 3, 0), ("A4", 3, 1), ("A3", 1, 1), ("F1", 0, 0), ("A2", 6, 0), ("A2", 6, 1),
    ("A5", 1, 0), ("E", 5, 0), ("A1", 4, 0), ("A2", 2, 0), ("F2", 0, 0), ("A2", 2, 1),
    ("A3", 4, 1), ("E", 7, 0), ("A5", 3, 0), ("A5", 3, 1), ("A4", 1, 1), ("A3", 6, 0),
    ("A3", 6, 1), ("A2", 5, 0), ("A2", 4, 0), ("A3", 2, 0), ("A3", 2, 1), ("A4", 4, 1),
    ("A2", 7, 0), ("F1", 1, 0), ("A4", 6, 0), ("A4", 6, 1), ("A3", 5, 0), ("A1", 5, 1),
    ("C", 1, 0), ("W", 1, 0), ("A3", 4, 0), ("F2", 1, 0), ("F1", 3, 0), ("A5", 4, 1),
    ("A4", 2, 0), ("A4", 2, 1), ("A1", 7, 1), ("A3", 7, 0), ("A5", 6, 0), ("W", 1, 1),
    ("A5", 6, 1), ("A4", 5, 0), ("F2", 3, 0), ("A2", 5, 1), ("A4", 4, 0), ("F1", 2, 0),
    ("A2", 7, 1), ("C", 3, 0), ("A5", 5, 0), ("A4", 7, 0), ("W", 3, 0), ("A3", 5, 1),
    ("F2", 2, 0), ("F1", 4, 0), ("A3", 7, 1), ("A5", 7, 0), ("F1", 6, 0), ("A4", 5, 1),
    ("F2", 4, 0), ("W", 3, 1), ("A4", 7, 1), ("F2", 6, 0), ("F1", 5, 0), ("F1", 7, 0),
    ("C", 5, 0), ("F2", 5, 0), ("W", 5, 0), ("F2", 7, 0), ("FX", 0, 0), ("W", 5, 1),
    ("C", 7, 0), ("W", 7, 0), ("W", 7, 1), ("END", 0, 0),
)


def gelu_both(v):
    t = jnp.tanh(gelu_scale * (v + gelu_cubic * v * v * v))
    value = 0.5 * v * (1.0 + t)
    slope = 0.5 * (1.0 + t) + 0.5 * v * (1.0 - t * t) * gelu_scale * (
        1.0 + 3.0 * gelu_cubic * v * v
    )
    return value, slope


def dot_nn(left, right):
    return jnp.dot(left, right, preferred_element_type=F32)


def dot_nt(left, right):
    return lax.dot_general(left, right, (((1,), (1,)), ((), ())), preferred_element_type=F32)


def kernel(
    tok_ref, wup_ref, bup_ref, wdn_ref, bdn_ref, cot_ref,
    out_ref, gtok_ref, gwu_ref, gbu_ref, gwd_ref, gbd_ref,
    tc, tct, part, zland, xland, own, full, acc_u, acc_d,
    opart, rcore, sy, ry, sx, rx, cs, bs, ball, brow,
    rzs, rzr, azs, azr, rxs, rxr, axs, axr, hs, hr, fs, fr, bzs, bzr,
):
    gx, gy, gz = lax.axis_index("gx"), lax.axis_index("gy"), lax.axis_index("gz")
    z, xl = lax.rem(gz, NZ), lax.div(gz, NZ)
    xh, core = lax.div(gx, 2), lax.rem(gx, 2)
    feat, width = wup_ref.shape
    half = width // 2
    rows = tok_ref.shape[0]
    crow = 2 * rows
    unit = crow // NZ

    def zi(j):
        return lax.rem(z + j + NZ, NZ)

    def side(x, shift, size):
        return pl.ds(pl.multiple_of(x * half + shift, 128), size)

    mine, theirs = side(xl, 0, half), side(1 - xl, 0, half)
    zdev = ({"gz": xl * NZ + zi(1)}, {"gz": xl * NZ + zi(-1)})
    xdev = {"gz": (1 - xl) * NZ + z}
    coredev = {"gx": xh * 2 + 1 - core}
    xhdev = {"gx": (1 - xh) * 2 + core}

    def ydev(d):
        return {"gy": lax.rem(gy + d + 4, 4)}

    def rcopy(src, dst, ss, rs, dev):
        return pltpu.make_async_remote_copy(
            src_ref=src, dst_ref=dst, send_sem=ss, recv_sem=rs,
            device_id=dev, device_id_type=MESH,
        )

    sent = []
    now = [0]

    def start(copy):
        copy.start()
        sent.append((now[0], copy))

    def rs_part(op, c, r, d):
        wide = half if RS_X[op][c] else width
        return (d * wide // 2, wide // 2) if r == 1 else (0, wide)

    def rs_unit(op, c, t, shift, size):
        cols = side(xl, shift, size) if RS_X[op][c] else pl.ds(shift, size)
        return part.at[op, c, t, :, cols]

    def rs_copy(op, c, r, d):
        shift, size = rs_part(op, c, r, d)
        return rcopy(
            rs_unit(op, c, zi(SIGN[d] * (5 - r)), shift, size),
            zland.at[op, c, d, r - 1, :, pl.ds(shift, size)],
            rzs.at[op, c, d * 4 + r - 1], rzr.at[op, c, d * 4 + r - 1], zdev[d],
        )

    def rs_step(op, c, r):
        for d in range(2):
            rs_copy(op, c, r - 1, d).wait_recv()
            shift, size = rs_part(op, c, r - 1, d)
            dst = rs_unit(op, c, zi(SIGN[d] * (5 - r)), shift, size)
            got = zland[op, c, d, r - 2, :, shift:shift + size]
            dst[...] = (dst[...].astype(F32) + got.astype(F32)).astype(BF)
            start(rs_copy(op, c, r, d))

    def rs_x(op, c):
        if RS_X[op][c]:
            src, dst = part.at[op, c, :, :, theirs], xland.at[op, c]
        else:
            src, dst = part.at[op, c, z, :, theirs], xland.at[op, c, 0]
        return rcopy(src, dst, rxs.at[op, c], rxr.at[op, c], xdev)

    def rs_total(op, c, cols, land):
        return (
            part[op, c, z, :, cols].astype(F32)
            + zland[op, c, 0, 3, :, land].astype(F32)
            + zland[op, c, 1, 3, :, land].astype(F32)
        )

    def ag_copy(op, c, r, d, arriving):
        t = zi(-SIGN[d] * (r if arriving else r - 1))
        wide = half if AG_X[op][c] else width
        shift, size = (d * wide // 2, wide // 2) if r == 4 else (0, wide)
        cols = side(xl, shift, size) if AG_X[op][c] else pl.ds(shift, size)
        ref = full.at[op, c, t, :, cols]
        k = d * 4 + r - 1
        return rcopy(ref, ref, azs.at[op, c, k], azr.at[op, c, k], zdev[d])

    def ag_x(op, c, j, arriving):
        ref = full.at[op, c, zi(j), :, theirs if arriving else mine]
        return rcopy(ref, ref, axs.at[op, c, j], axr.at[op, c, j], xdev)

    def bias_x(arriving):
        ref = ball.at[z, 1 - xl if arriving else xl]
        return rcopy(ref, ref, bzs.at[0], bzr.at[0], xdev)

    def bias_copy(r, d, arriving):
        ref = ball.at[zi(-SIGN[d] * (r if arriving else r - 1))]
        k = d * 4 + r
        return rcopy(ref, ref, bzs.at[k], bzr.at[k], zdev[d])

    chunk_of = {pair: c for c, pair in enumerate(CHUNKS)}
    own_rows = tc.at[:, 0, core]
    last = chunk_of[(0, 1)]
    other_rows = tc.at[:, last, core]

    def h_copy(k, src, dst, dev):
        return rcopy(src, dst, hs.at[k], hr.at[k], dev)

    def h_xh():
        return h_copy(0, own_rows, other_rows, xhdev)

    def h_y(c):
        u, h = CHUNKS[c]
        return h_copy(c, other_rows if h else own_rows, tc.at[:, c, core], ydev(-u))

    def h_core(c):
        ref = tc.at[:, c, core]
        return h_copy(NC + c, ref, ref, coredev)

    def f_core(c):
        return rcopy(opart.at[c, :, 1 - core], rcore.at[c], fs.at[0, c], fr.at[0, c], coredev)

    def f_y(c):
        return rcopy(sy.at[c], ry.at[c], fs.at[1, c], fr.at[1, c], ydev(CHUNKS[c][0]))

    def f_xh():
        return rcopy(sx, rx, fs.at[0, NC], fr.at[0, NC], xhdev)

    def ry_sum(h):
        picks = [c for c in range(NC) if CHUNKS[c][1] == h]
        for c in picks:
            if CHUNKS[c][0]:
                f_y(c).wait_recv()
        a, b, c, d = [ry[p].astype(F32) for p in picks]
        return (a + b) + (c + d)

    def b_y(d, arriving):
        ref = bs.at[lax.rem(gy - d + 4, 4) if arriving else gy]
        return rcopy(ref, ref, hs.at[2 * NC + d - 1], hr.at[2 * NC + d - 1], ydev(d))

    def ev_H(c, op):
        start(h_xh())
        start(h_core(0))
        for k in (1, 3, 5):
            start(h_y(k))
        start(bias_x(False))

    def ev_HX(c, op):
        h_xh().wait_recv()
        start(h_core(last))
        for k in (2, 4, 6):
            start(h_y(k))

    def ev_HF(c, op):
        h_y(c).wait_recv()
        start(h_core(c))

    arrived = set()

    def ev_PP(c, op):
        if c not in arrived:
            arrived.add(c)
            ref = tc.at[:, c, 1 - core]
            h_copy(NC + c, ref, ref, coredev).wait_recv()
        x = tc[op, c].reshape(crow, feat)

        @pl.loop(0, 2)
        def _(j):
            cols = pl.ds(pl.multiple_of(j * half, half), half)
            v = dot_nt(x, wdn_ref[cols, :]) if op == GRAD else dot_nn(x, wup_ref[:, cols])
            part[op, c, :, :, cols] = v.astype(BF).reshape(NZ, unit, half)

        if RS_X[op][c]:
            start(rs_x(op, c))
        else:
            for d in range(2):
                start(rs_copy(op, c, 1, d))

    def ev_R1(c, op):
        rs_x(op, c).wait_recv()
        part[op, c, :, :, mine] = (
            part[op, c, :, :, mine].astype(F32) + xland[op, c].astype(F32)
        ).astype(BF)
        for d in range(2):
            start(rs_copy(op, c, 1, d))

    def ev_R5(c, op):
        for d in range(2):
            rs_copy(op, c, 4, d).wait_recv()
        part[op, c, z, :, theirs] = rs_total(op, c, theirs, theirs).astype(BF)
        start(rs_x(op, c))
        own[op, c] = rs_total(op, c, mine, mine)

    def ev_E(c, op):
        got = []
        for o in (PRE, GRAD):
            if RS_X[o][c]:
                for d in range(2):
                    rs_copy(o, c, 4, d).wait_recv()
                got.append(rs_total(o, c, mine, pl.ds(0, half)))
            else:
                rs_x(o, c).wait_recv()
                got.append(own[o, c] + xland[o, c, 0].astype(F32))
        value, slope = gelu_both(got[PRE] + brow[0:1, :])
        full[PRE, c, z, :, mine] = value.astype(BF)
        full[GRAD, c, z, :, mine] = (got[GRAD] * slope).astype(BF)
        for o in (PRE, GRAD):
            if AG_X[o][c]:
                for d in range(2):
                    start(ag_copy(o, c, 1, d, False))
            start(ag_x(o, c, 0, False))

    def ev_A1(c, op):
        ag_x(op, c, 0, True).wait_recv()
        for d in range(2):
            start(ag_copy(op, c, 1, d, False))

    def ag_step(c, op, r):
        for d in range(2):
            ag_copy(op, c, r - 1, d, True).wait_recv()
            start(ag_copy(op, c, r, d, False))
            if AG_X[op][c]:
                start(ag_x(op, c, (-SIGN[d] * (r - 1)) % NZ, False))

    def ev_A5(c, op):
        for d in range(2):
            ag_copy(op, c, 4, d, True).wait_recv()
        start(ag_x(op, c, 4, False))

    def ev_F1(c, op):
        for o in (PRE, GRAD):
            if AG_X[o][c]:
                for j in range(NZ):
                    ag_x(o, c, j, True).wait_recv()
            else:
                for d in range(2):
                    ag_copy(o, c, 4, d, True).wait_recv()
        v = dot_nn(full[PRE, c].reshape(crow, width), wdn_ref[...])
        opart[c, 0] = v.astype(BF).reshape(2, rows, feat)
        v = dot_nt(full[GRAD, c].reshape(crow, width), wup_ref[...])
        opart[c, 1] = v.astype(BF).reshape(2, rows, feat)
        start(f_core(c))

    def ev_F2(c, op):
        f_core(c).wait_recv()
        v = (opart[c, :, core].astype(F32) + rcore[c].astype(F32)).astype(BF)
        if CHUNKS[c][0]:
            sy[c] = v
            start(f_y(c))
        else:
            ry[c] = v

    def ev_FX(c, op):
        sx[...] = ry_sum(1).astype(BF)
        start(f_xh())

    def ev_W(c, op):
        p = c // 2
        acc, out, other = ((acc_u, gwu_ref, GRAD), (acc_d, None, PRE))[op]
        tct[op, p] = tc[op, c - 1:c + 1].reshape(2 * crow, feat).T

        @pl.loop(0, 3)
        def _(j):
            cols = pl.ds(pl.multiple_of(j * 512, 512), 512)
            v = dot_nn(tct[op, p], full[other, c - 1:c + 1, :, :, cols].reshape(2 * crow, 512))
            if p:
                v += acc[:, cols]
            if c == NC - 1 and op == PRE:
                gwu_ref[:, cols] = v.astype(BF)
            else:
                acc[:, cols] = v

        if c == NC - 1 and op == GRAD:
            gwd_ref[...] = acc_d[...].astype(BF).T

    def ev_C(c, op):
        v = full[GRAD, c - 1:c + 1].reshape(2 * crow // 8, 8, width).astype(F32)
        v = jnp.sum(v, axis=0)
        if c > 1:
            v += cs[...]
        cs[...] = v
        if c == NC - 1:
            piece = pl.ds(pl.multiple_of(lax.rem(gz, 4) * feat, 128), feat)
            bs[gy] = cs[:, piece]
            for d in (1, 2, 3):
                start(b_y(d, False))

    def ev_D(c, op):
        gbd_ref[...] = jnp.sum(tc[1].reshape(NC * crow, feat).astype(F32), axis=0)

    def bias_step(r):
        if r == 1:
            bias_x(True).wait_recv()
        else:
            for d in range(2):
                if r < 5 or d == 0:
                    bias_copy(r - 1, d, True).wait_recv()
        if r < 5:
            for d in range(2):
                if r < 4 or d == 0:
                    start(bias_copy(r, d, False))
        else:
            for j in range(2):
                piece = gy * 4 + xl * 2 + j
                brow[:, j * feat:(j + 1) * feat] = ball[lax.rem(piece, NZ), lax.div(piece, NZ)]

    def ev_END(c, op):
        for d in (1, 2, 3):
            b_y(d, True).wait_recv()
        gbu_ref[...] = jnp.sum(bs[lax.div(gz, 4)], axis=0)
        total = ry_sum(0)
        f_xh().wait_recv()
        total += rx[...].astype(F32)
        out_ref[...] = (total[0] + bdn_ref[...][None, :]).astype(BF)
        gtok_ref[...] = total[1].astype(BF)

    events = {
        "H": ev_H, "HX": ev_HX, "HF": ev_HF, "PP": ev_PP, "R1": ev_R1, "R5": ev_R5,
        "E": ev_E, "A1": ev_A1, "A5": ev_A5, "F1": ev_F1, "F2": ev_F2, "FX": ev_FX,
        "W": ev_W, "C": ev_C, "D": ev_D, "END": ev_END,
    }

    for i, ref in enumerate((tok_ref, cot_ref)):
        tc[i, 0, core] = ref[...]
    ball[z, xl] = jnp.broadcast_to(bup_ref[...][None, :], ball.shape[2:])

    barrier = pltpu.get_barrier_semaphore()
    peers = (zdev[0], zdev[1], xdev, coredev, xhdev, ydev(1), ydev(2), ydev(3))
    for dev in peers:
        pl.semaphore_signal(barrier, inc=1, device_id=dev, device_id_type=MESH)
    pl.semaphore_wait(barrier, len(peers))

    for now[0], (kind, c, op) in enumerate(ORDER):
        if kind in ("R2", "R3", "R4"):
            rs_step(op, c, int(kind[1]))
        elif kind in ("A2", "A3", "A4"):
            ag_step(c, op, int(kind[1]))
        elif kind[0] == "B":
            bias_step(int(kind[1]))
        else:
            events[kind](c, op)
        while sent and sent[0][0] <= now[0] - LAG:
            sent.pop(0)[1].wait_send()
    for _, copy in sent:
        copy.wait_send()


def per_device(tokens, w_up, b_up, w_down, b_down, cotangent):
    rows, feat = tokens.shape
    width = w_up.shape[1]
    half = width // 2
    unit = 2 * rows // NZ
    vmem = pl.BlockSpec(memory_space=pltpu.VMEM)
    dma = pltpu.SemaphoreType.DMA
    scratch = [
        pltpu.VMEM((2, NC, 2, rows, feat), BF),
        pltpu.VMEM((2, NC // 2, feat, 4 * rows), BF),
        pltpu.VMEM((2, NC, NZ, unit, width), BF),
        pltpu.VMEM((2, NC, 2, 4, unit, width), BF),
        pltpu.VMEM((2, NC, NZ, unit, half), BF),
        pltpu.VMEM((2, NC, unit, half), F32),
        pltpu.VMEM((2, NC, NZ, unit, width), BF),
        pltpu.VMEM((feat, width), F32),
        pltpu.VMEM((feat, width), F32),
        pltpu.VMEM((NC, 2, 2, rows, feat), BF),
        pltpu.VMEM((NC, 2, rows, feat), BF),
        pltpu.VMEM((NC, 2, rows, feat), BF),
        pltpu.VMEM((NC, 2, rows, feat), BF),
        pltpu.VMEM((2, rows, feat), BF),
        pltpu.VMEM((2, rows, feat), BF),
        pltpu.VMEM((8, width), F32),
        pltpu.VMEM((4, 8, feat), F32),
        pltpu.VMEM((NZ, 2, 8, feat), F32),
        pltpu.VMEM((8, half), F32),
        dma((2, NC, 8)), dma((2, NC, 8)),
        dma((2, NC, 8)), dma((2, NC, 8)),
        dma((2, NC)), dma((2, NC)),
        dma((2, NC, NZ)), dma((2, NC, NZ)),
        dma((2 * NC + 3,)), dma((2 * NC + 3,)),
        dma((2, NC + 1)), dma((2, NC + 1)),
        dma((9,)), dma((9,)),
    ]
    return pl.pallas_call(
        kernel,
        out_shape=(
            jax.ShapeDtypeStruct((rows, feat), BF),
            jax.ShapeDtypeStruct((rows, feat), BF),
            jax.ShapeDtypeStruct((feat, width), BF),
            jax.ShapeDtypeStruct((feat,), F32),
            jax.ShapeDtypeStruct((width, feat), BF),
            jax.ShapeDtypeStruct((feat,), F32),
        ),
        in_specs=[vmem] * 6,
        out_specs=(vmem,) * 6,
        scratch_shapes=scratch,
        compiler_params=pltpu.CompilerParams(
            collective_id=0, has_side_effects=True, vmem_limit_bytes=60 * 2**20
        ),
        name="mlp_block",
    )(tokens, w_up, b_up, w_down, b_down, cotangent)


def solution(mesh):
    rows = P(("gx", "gy"), "gz")
    up = P("gz", ("gx", "gy"))
    down = P(("gx", "gy"), "gz")
    return jax.shard_map(
        per_device,
        mesh=mesh,
        in_specs=(rows, up, P(("gx", "gz")), down, P("gz"), rows),
        out_specs=(rows, rows, up, P(("gx", "gz")), down, P("gz")),
        check_vma=False,
    )
```

time: 514 us -> 133 us (0.26)
  waiting for transfers between devices: 347 us -> 0 us
  Pallas kernels: 0 us -> 125 us
  blocking collectives: 115 us -> 0 us
  matrix products: 25.4 us -> 0 us
  between operations: 14.2 us -> 0.65 us
  other arithmetic: 6.78 us -> 0 us
    reduce_scatter x4 -> x0, waiting for transfers between devices: 206 us -> none  [the longest x1 76.4 us: per_device(): lax.psum_scatter(contract_cols(grad, w_up).astype(jnp.bfloat16), rows_axe...]
    all_gather x2 -> x0, waiting for transfers between devices: 141 us -> none  [the longest x1 71.6 us: per_device(): act = lax.all_gather(value.astype(jnp.bfloat16), 'gz', axis=0, tiled=True)]
    pallas_call x0 -> x1, Pallas kernels: none -> 125 us  [per_device(): pl.pallas_call(kernel, out_shape=(jax.ShapeDtypeStruct((rows, feat), BF),...]
    all_gather x4 -> x0, blocking collectives: 115 us -> none  [the longest x2 75.7 us: per_device(): lax.all_gather((tokens, cotangent), rows_axes, axis=0, tiled=True)]
    dot_general x6 -> x0, matrix products: 25.4 us -> none  [the longest x2 8.09 us: contract_cols(): lax.dot_general(left, right, (((1,), (1,)), ((), ())), preferred_element_...]
  transfers between devices with their start and end apart: 6 -> 0, of which waited for: 5 -> 0; matrix products, arithmetic and copies ran while one was open for 5% -> 0% of each run, Pallas kernels for 0% -> 0%
where the time goes in v3:
time: 133 us
  Pallas kernels  125 us (94%)
  local copies, waits for them, and re-layouts  7.48 us (6%)
    pallas_call x1, Pallas kernels, per_device(): pl.pallas_call(kernel, out_shape=(jax.ShapeDtypeStruct((rows, feat), BF),...  125 us
    unnamed x12, local copies, waits for them, and re-layouts  7.48 us

profile of v3, /device:TPU:1, one launch (start us, length us, event | category | flops | bytes accessed | tf_op | source)
XLA Modules:
  0.0 132.8 jit_solution(17191711002388650083)
XLA Ops:
  0.6 124.7 %mlp_block.1 = (bf16[64,384]{1,0:T(8,128)(2,1)}, bf16[64,384]{1,0:T(8,128)(2,1)}, bf16[384,1536]{1,0:T(8,128)(2,1)}, f32[384]{0:T(512)}, bf16[1536,384]{1,0:T(8,128)(2,1)}, /*index=5*/f32[384]{0:T(512)}) custom-call(bf16[64,384]{1,0:T(8,128)(2,1)} %tok_ref.1, bf16[384,1536]{1,0:T(8,128)(2,1)} %wup_ref.1, f32[384]{0:T(512)} %bup_ref.1, ...), custom_call_target="tpu_custom_call" | custom-call | tf_op jit(solution)/shard_map/mlp_block/pallas_call | solution.py:463
  125.4 1.4 %copy.18 = bf16[64,384]{1,0:T(8,128)(2,1)} copy(bf16[64,384]{1,0:T(8,128)(2,1)} %get-tuple-element.12) | data formatting | bytes 98304
  126.8 1.4 %copy.19 = bf16[64,384]{1,0:T(8,128)(2,1)} copy(bf16[64,384]{1,0:T(8,128)(2,1)} %get-tuple-element.13) | data formatting | bytes 98304
  128.2 0.0 copy-start.2
  128.2 0.0 copy-start
  128.2 2.5 %copy.20 = bf16[384,1536]{1,0:T(8,128)(2,1)} copy(bf16[384,1536]{1,0:T(8,128)(2,1)} %get-tuple-element.14) | data formatting | bytes 2359296
  130.7 0.0 copy-done.2
  130.7 0.6 copy.21
  131.2 0.0 copy-done
  131.2 0.0 copy-start.1
  131.3 1.0 copy.22
  132.3 0.0 copy-done.1
  132.3 0.6 copy.23
Async XLA Ops:
  128.2 2.5 %copy-start.2 = (f32[384]{0:T(512)S(1)}, f32[384]{0:T(512)}, u32[]{:S(2)}) copy-start(f32[384]{0:T(512)} %get-tuple-element.15) | copy-start | bytes 4612
  128.2 3.0 %copy-start = (bf16[1536,384]{1,0:T(8,128)(2,1)S(1)}, bf16[1536,384]{1,0:T(8,128)(2,1)}, u32[]{:S(2)}) copy-start(bf16[1536,384]{1,0:T(8,128)(2,1)} %get-tuple-element.16) | copy-start | bytes 3538948
  131.2 1.0 copy-start.1

commit v4 on v3

--- a/solution.py
+++ b/solution.py
@@ -15,7 +15,7 @@
 NC = len(CHUNKS)
 SIGN = (1, -1)
 PRE, GRAD = 0, 1
-LAG = 30
+Z_POOL, X_POOL, POOL = 64, 64, 32
 
 RS_X = ((1, 1, 0, 1, 1, 1, 0, 1), (0, 0, 1, 0, 1, 1, 0, 0))
 AG_X = ((1, 1, 0, 1, 0, 1, 1, 1), (1, 0, 0, 1, 1, 0, 1, 0))
@@ -74,16 +74,17 @@
 
 
 def kernel(
-    tok_ref, wup_ref, bup_ref, wdn_ref, bdn_ref, cot_ref,
-    out_ref, gtok_ref, gwu_ref, gbu_ref, gwd_ref, gbd_ref,
+    tok_ref, wup_hbm, bup_ref, wdn_hbm, bdn_ref, cot_ref,
+    out_ref, gtok_ref, gwu_hbm, gbu_ref, gwd_hbm, gbd_ref,
     tc, tct, part, zland, xland, own, full, acc_u, acc_d,
     opart, rcore, sy, ry, sx, rx, cs, bs, ball, brow,
-    rzs, rzr, azs, azr, rxs, rxr, axs, axr, hs, hr, fs, fr, bzs, bzr,
+    wup_vm, wdn_vm, gwu_vm, gwd_vm,
+    rzr, azr, rxr, axr, hr, fr, bzr, zpool, xpool, pool, ls,
 ):
     gx, gy, gz = lax.axis_index("gx"), lax.axis_index("gy"), lax.axis_index("gz")
     z, xl = lax.rem(gz, NZ), lax.div(gz, NZ)
     xh, core = lax.div(gx, 2), lax.rem(gx, 2)
-    feat, width = wup_ref.shape
+    feat, width = wup_vm.shape
     half = width // 2
     rows = tok_ref.shape[0]
     crow = 2 * rows
@@ -104,18 +105,29 @@
     def ydev(d):
         return {"gy": lax.rem(gy + d + 4, 4)}
 
-    def rcopy(src, dst, ss, rs, dev):
+    def rcopy(message, send_sem):
+        src, dst, recv_sem, dev = message
         return pltpu.make_async_remote_copy(
-            src_ref=src, dst_ref=dst, send_sem=ss, recv_sem=rs,
+            src_ref=src, dst_ref=dst, send_sem=send_sem, recv_sem=recv_sem,
             device_id=dev, device_id_type=MESH,
         )
 
-    sent = []
-    now = [0]
-
-    def start(copy):
-        copy.start()
-        sent.append((now[0], copy))
+    slots = {id(p): ([None] * p.shape[0], [0]) for p in (zpool, xpool, pool)}
+
+    def start(message, sems):
+        held, count = slots[id(sems)]
+        k = count[0] % len(held)
+        count[0] += 1
+        if held[k] is not None:
+            held[k].wait_send()
+        held[k] = rcopy(message, sems.at[k])
+        held[k].start()
+
+    def arrive(message):
+        rcopy(message, pool.at[0]).wait_recv()
+
+    def arrive_all(like, sem):
+        pltpu.make_async_copy(like, like, sem).wait()
 
     def rs_part(op, c, r, d):
         wide = half if RS_X[op][c] else width
@@ -127,27 +139,32 @@
 
     def rs_copy(op, c, r, d):
         shift, size = rs_part(op, c, r, d)
-        return rcopy(
+        return (
             rs_unit(op, c, zi(SIGN[d] * (5 - r)), shift, size),
             zland.at[op, c, d, r - 1, :, pl.ds(shift, size)],
-            rzs.at[op, c, d * 4 + r - 1], rzr.at[op, c, d * 4 + r - 1], zdev[d],
+            rzr.at[op, c, r - 1], zdev[d],
         )
 
+    def rs_arrive(op, c, r):
+        wide = half if RS_X[op][c] else width
+        like = zland.at[op, c, :, r - 1, :, pl.ds(0, wide // 2 if r == 1 else wide)]
+        arrive_all(like, rzr.at[op, c, r - 1])
+
     def rs_step(op, c, r):
+        rs_arrive(op, c, r - 1)
         for d in range(2):
-            rs_copy(op, c, r - 1, d).wait_recv()
             shift, size = rs_part(op, c, r - 1, d)
             dst = rs_unit(op, c, zi(SIGN[d] * (5 - r)), shift, size)
             got = zland[op, c, d, r - 2, :, shift:shift + size]
             dst[...] = (dst[...].astype(F32) + got.astype(F32)).astype(BF)
-            start(rs_copy(op, c, r, d))
+            start(rs_copy(op, c, r, d), zpool)
 
     def rs_x(op, c):
         if RS_X[op][c]:
             src, dst = part.at[op, c, :, :, theirs], xland.at[op, c]
         else:
             src, dst = part.at[op, c, z, :, theirs], xland.at[op, c, 0]
-        return rcopy(src, dst, rxs.at[op, c], rxr.at[op, c], xdev)
+        return src, dst, rxr.at[op, c], xdev
 
     def rs_total(op, c, cols, land):
         return (
@@ -156,27 +173,29 @@
             + zland[op, c, 1, 3, :, land].astype(F32)
         )
 
-    def ag_copy(op, c, r, d, arriving):
-        t = zi(-SIGN[d] * (r if arriving else r - 1))
+    def ag_copy(op, c, r, d):
+        t = zi(-SIGN[d] * (r - 1))
         wide = half if AG_X[op][c] else width
         shift, size = (d * wide // 2, wide // 2) if r == 4 else (0, wide)
         cols = side(xl, shift, size) if AG_X[op][c] else pl.ds(shift, size)
         ref = full.at[op, c, t, :, cols]
-        k = d * 4 + r - 1
-        return rcopy(ref, ref, azs.at[op, c, k], azr.at[op, c, k], zdev[d])
-
-    def ag_x(op, c, j, arriving):
-        ref = full.at[op, c, zi(j), :, theirs if arriving else mine]
-        return rcopy(ref, ref, axs.at[op, c, j], axr.at[op, c, j], xdev)
-
-    def bias_x(arriving):
-        ref = ball.at[z, 1 - xl if arriving else xl]
-        return rcopy(ref, ref, bzs.at[0], bzr.at[0], xdev)
-
-    def bias_copy(r, d, arriving):
-        ref = ball.at[zi(-SIGN[d] * (r if arriving else r - 1))]
-        k = d * 4 + r
-        return rcopy(ref, ref, bzs.at[k], bzr.at[k], zdev[d])
+        return ref, ref, azr.at[op, c, r - 1], zdev[d]
+
+    def ag_arrive(op, c, r):
+        wide = half if AG_X[op][c] else width
+        like = zland.at[op, c, :, 0, :, pl.ds(0, wide // 2 if r == 4 else wide)]
+        arrive_all(like, azr.at[op, c, r - 1])
+
+    def ag_x(op, c, j):
+        ref = full.at[op, c, zi(j), :, mine]
+        return ref, ref, axr.at[op, c], xdev
+
+    def bias_x():
+        return ball.at[z, xl], ball.at[z, xl], bzr.at[0], xdev
+
+    def bias_copy(r, d):
+        ref = ball.at[zi(-SIGN[d] * (r - 1))]
+        return ref, ref, bzr.at[r], zdev[d]
 
     chunk_of = {pair: c for c, pair in enumerate(CHUNKS)}
     own_rows = tc.at[:, 0, core]
@@ -184,7 +203,7 @@
     other_rows = tc.at[:, last, core]
 
     def h_copy(k, src, dst, dev):
-        return rcopy(src, dst, hs.at[k], hr.at[k], dev)
+        return src, dst, hr.at[k], dev
 
     def h_xh():
         return h_copy(0, own_rows, other_rows, xhdev)
@@ -198,88 +217,86 @@
         return h_copy(NC + c, ref, ref, coredev)
 
     def f_core(c):
-        return rcopy(opart.at[c, :, 1 - core], rcore.at[c], fs.at[0, c], fr.at[0, c], coredev)
+        return opart.at[c, :, 1 - core], rcore.at[c], fr.at[0, c], coredev
 
     def f_y(c):
-        return rcopy(sy.at[c], ry.at[c], fs.at[1, c], fr.at[1, c], ydev(CHUNKS[c][0]))
+        return sy.at[c], ry.at[c], fr.at[1, c], ydev(CHUNKS[c][0])
 
     def f_xh():
-        return rcopy(sx, rx, fs.at[0, NC], fr.at[0, NC], xhdev)
+        return sx, rx, fr.at[0, NC], xhdev
 
     def ry_sum(h):
         picks = [c for c in range(NC) if CHUNKS[c][1] == h]
         for c in picks:
             if CHUNKS[c][0]:
-                f_y(c).wait_recv()
+                arrive(f_y(c))
         a, b, c, d = [ry[p].astype(F32) for p in picks]
         return (a + b) + (c + d)
 
-    def b_y(d, arriving):
-        ref = bs.at[lax.rem(gy - d + 4, 4) if arriving else gy]
-        return rcopy(ref, ref, hs.at[2 * NC + d - 1], hr.at[2 * NC + d - 1], ydev(d))
+    def b_y(d):
+        return bs.at[gy], bs.at[gy], hr.at[2 * NC], ydev(d)
 
     def ev_H(c, op):
-        start(h_xh())
-        start(h_core(0))
+        start(h_core(0), pool)
+        start(h_xh(), pool)
         for k in (1, 3, 5):
-            start(h_y(k))
-        start(bias_x(False))
+            start(h_y(k), pool)
+        start(bias_x(), xpool)
 
     def ev_HX(c, op):
-        h_xh().wait_recv()
-        start(h_core(last))
+        arrive(h_xh())
+        start(h_core(last), pool)
         for k in (2, 4, 6):
-            start(h_y(k))
+            start(h_y(k), pool)
 
     def ev_HF(c, op):
-        h_y(c).wait_recv()
-        start(h_core(c))
+        arrive(h_y(c))
+        start(h_core(c), pool)
 
     arrived = set()
 
     def ev_PP(c, op):
         if c not in arrived:
             arrived.add(c)
-            ref = tc.at[:, c, 1 - core]
-            h_copy(NC + c, ref, ref, coredev).wait_recv()
+            arrive(h_core(c))
+        if c == 0:
+            local(0 if op == GRAD else 1).wait()
         x = tc[op, c].reshape(crow, feat)
 
         @pl.loop(0, 2)
         def _(j):
             cols = pl.ds(pl.multiple_of(j * half, half), half)
-            v = dot_nt(x, wdn_ref[cols, :]) if op == GRAD else dot_nn(x, wup_ref[:, cols])
+            v = dot_nt(x, wdn_vm[cols, :]) if op == GRAD else dot_nn(x, wup_vm[:, cols])
             part[op, c, :, :, cols] = v.astype(BF).reshape(NZ, unit, half)
 
         if RS_X[op][c]:
-            start(rs_x(op, c))
+            start(rs_x(op, c), xpool)
         else:
             for d in range(2):
-                start(rs_copy(op, c, 1, d))
+                start(rs_copy(op, c, 1, d), zpool)
 
     def ev_R1(c, op):
-        rs_x(op, c).wait_recv()
+        arrive(rs_x(op, c))
         part[op, c, :, :, mine] = (
             part[op, c, :, :, mine].astype(F32) + xland[op, c].astype(F32)
         ).astype(BF)
         for d in range(2):
-            start(rs_copy(op, c, 1, d))
+            start(rs_copy(op, c, 1, d), zpool)
 
     def ev_R5(c, op):
-        for d in range(2):
-            rs_copy(op, c, 4, d).wait_recv()
+        rs_arrive(op, c, 4)
         part[op, c, z, :, theirs] = rs_total(op, c, theirs, theirs).astype(BF)
-        start(rs_x(op, c))
+        start(rs_x(op, c), xpool)
         own[op, c] = rs_total(op, c, mine, mine)
 
     def ev_E(c, op):
         got = []
         for o in (PRE, GRAD):
             if RS_X[o][c]:
-                for d in range(2):
-                    rs_copy(o, c, 4, d).wait_recv()
+                rs_arrive(o, c, 4)
                 got.append(rs_total(o, c, mine, pl.ds(0, half)))
             else:
-                rs_x(o, c).wait_recv()
+                arrive(rs_x(o, c))
                 got.append(own[o, c] + xland[o, c, 0].astype(F32))
         value, slope = gelu_both(got[PRE] + brow[0:1, :])
         full[PRE, c, z, :, mine] = value.astype(BF)
@@ -287,56 +304,53 @@
         for o in (PRE, GRAD):
             if AG_X[o][c]:
                 for d in range(2):
-                    start(ag_copy(o, c, 1, d, False))
-            start(ag_x(o, c, 0, False))
+                    start(ag_copy(o, c, 1, d), zpool)
+            start(ag_x(o, c, 0), xpool)
 
     def ev_A1(c, op):
-        ag_x(op, c, 0, True).wait_recv()
+        arrive(ag_x(op, c, 0))
         for d in range(2):
-            start(ag_copy(op, c, 1, d, False))
+            start(ag_copy(op, c, 1, d), zpool)
 
     def ag_step(c, op, r):
+        ag_arrive(op, c, r - 1)
         for d in range(2):
-            ag_copy(op, c, r - 1, d, True).wait_recv()
-            start(ag_copy(op, c, r, d, False))
+            start(ag_copy(op, c, r, d), zpool)
             if AG_X[op][c]:
-                start(ag_x(op, c, (-SIGN[d] * (r - 1)) % NZ, False))
+                start(ag_x(op, c, (-SIGN[d] * (r - 1)) % NZ), xpool)
 
     def ev_A5(c, op):
-        for d in range(2):
-            ag_copy(op, c, 4, d, True).wait_recv()
-        start(ag_x(op, c, 4, False))
+        ag_arrive(op, c, 4)
+        start(ag_x(op, c, 4), xpool)
 
     def ev_F1(c, op):
         for o in (PRE, GRAD):
             if AG_X[o][c]:
-                for j in range(NZ):
-                    ag_x(o, c, j, True).wait_recv()
+                arrive_all(xland.at[o, c], axr.at[o, c])
             else:
-                for d in range(2):
-                    ag_copy(o, c, 4, d, True).wait_recv()
-        v = dot_nn(full[PRE, c].reshape(crow, width), wdn_ref[...])
+                ag_arrive(o, c, 4)
+        v = dot_nn(full[PRE, c].reshape(crow, width), wdn_vm[...])
         opart[c, 0] = v.astype(BF).reshape(2, rows, feat)
-        v = dot_nt(full[GRAD, c].reshape(crow, width), wup_ref[...])
+        v = dot_nt(full[GRAD, c].reshape(crow, width), wup_vm[...])
         opart[c, 1] = v.astype(BF).reshape(2, rows, feat)
-        start(f_core(c))
+        start(f_core(c), pool)
 
     def ev_F2(c, op):
-        f_core(c).wait_recv()
+        arrive(f_core(c))
         v = (opart[c, :, core].astype(F32) + rcore[c].astype(F32)).astype(BF)
         if CHUNKS[c][0]:
             sy[c] = v
-            start(f_y(c))
+            start(f_y(c), pool)
         else:
             ry[c] = v
 
     def ev_FX(c, op):
         sx[...] = ry_sum(1).astype(BF)
-        start(f_xh())
+        start(f_xh(), pool)
 
     def ev_W(c, op):
         p = c // 2
-        acc, out, other = ((acc_u, gwu_ref, GRAD), (acc_d, None, PRE))[op]
+        acc, out, other = ((acc_u, gwu_vm, GRAD), (acc_d, None, PRE))[op]
         tct[op, p] = tc[op, c - 1:c + 1].reshape(2 * crow, feat).T
 
         @pl.loop(0, 3)
@@ -346,12 +360,15 @@
             if p:
                 v += acc[:, cols]
             if c == NC - 1 and op == PRE:
-                gwu_ref[:, cols] = v.astype(BF)
+                gwu_vm[:, cols] = v.astype(BF)
             else:
                 acc[:, cols] = v
 
+        if c == NC - 1 and op == PRE:
+            local(2).start()
         if c == NC - 1 and op == GRAD:
-            gwd_ref[...] = acc_d[...].astype(BF).T
+            gwd_vm[...] = acc_d[...].astype(BF).T
+            local(3).start()
 
     def ev_C(c, op):
         v = full[GRAD, c - 1:c + 1].reshape(2 * crow // 8, 8, width).astype(F32)
@@ -363,33 +380,29 @@
             piece = pl.ds(pl.multiple_of(lax.rem(gz, 4) * feat, 128), feat)
             bs[gy] = cs[:, piece]
             for d in (1, 2, 3):
-                start(b_y(d, False))
+                start(b_y(d), pool)
 
     def ev_D(c, op):
         gbd_ref[...] = jnp.sum(tc[1].reshape(NC * crow, feat).astype(F32), axis=0)
 
     def bias_step(r):
         if r == 1:
-            bias_x(True).wait_recv()
+            arrive(bias_x())
         else:
-            for d in range(2):
-                if r < 5 or d == 0:
-                    bias_copy(r - 1, d, True).wait_recv()
+            arrive_all(ball.at[0:2 if r < 5 else 1], bzr.at[r - 1])
         if r < 5:
-            for d in range(2):
-                if r < 4 or d == 0:
-                    start(bias_copy(r, d, False))
+            for d in range(2 if r < 4 else 1):
+                start(bias_copy(r, d), zpool)
         else:
             for j in range(2):
                 piece = gy * 4 + xl * 2 + j
                 brow[:, j * feat:(j + 1) * feat] = ball[lax.rem(piece, NZ), lax.div(piece, NZ)]
 
     def ev_END(c, op):
-        for d in (1, 2, 3):
-            b_y(d, True).wait_recv()
+        arrive_all(bs.at[0:3], hr.at[2 * NC])
         gbu_ref[...] = jnp.sum(bs[lax.div(gz, 4)], axis=0)
         total = ry_sum(0)
-        f_xh().wait_recv()
+        arrive(f_xh())
         total += rx[...].astype(F32)
         out_ref[...] = (total[0] + bdn_ref[...][None, :]).astype(BF)
         gtok_ref[...] = total[1].astype(BF)
@@ -400,6 +413,14 @@
         "W": ev_W, "C": ev_C, "D": ev_D, "END": ev_END,
     }
 
+    def local(k):
+        src, dst = (
+            (wdn_hbm, wdn_vm), (wup_hbm, wup_vm), (gwu_vm, gwu_hbm), (gwd_vm, gwd_hbm),
+        )[k]
+        return pltpu.make_async_copy(src, dst, ls.at[k])
+
+    local(0).start()
+    local(1).start()
     for i, ref in enumerate((tok_ref, cot_ref)):
         tc[i, 0, core] = ref[...]
     ball[z, xl] = jnp.broadcast_to(bup_ref[...][None, :], ball.shape[2:])
@@ -410,7 +431,7 @@
         pl.semaphore_signal(barrier, inc=1, device_id=dev, device_id_type=MESH)
     pl.semaphore_wait(barrier, len(peers))
 
-    for now[0], (kind, c, op) in enumerate(ORDER):
+    for kind, c, op in ORDER:
         if kind in ("R2", "R3", "R4"):
             rs_step(op, c, int(kind[1]))
         elif kind in ("A2", "A3", "A4"):
@@ -419,10 +440,40 @@
             bias_step(int(kind[1]))
         else:
             events[kind](c, op)
-        while sent and sent[0][0] <= now[0] - LAG:
-            sent.pop(0)[1].wait_send()
-    for _, copy in sent:
-        copy.wait_send()
+    for held, _ in slots.values():
+        for copy in held:
+            if copy is not None:
+                copy.wait_send()
+    local(2).wait()
+    local(3).wait()
+
+
+def hand_over(results):
+    count = len(results)
+
+    def move(*refs):
+        source, target, held = refs[:count], refs[count:2 * count], refs[2 * count:3 * count]
+        sems = refs[3 * count]
+        first = [pltpu.make_async_copy(source[k], held[k], sems.at[0, k]) for k in range(count)]
+        second = [pltpu.make_async_copy(held[k], target[k], sems.at[1, k]) for k in range(count)]
+        for copy in first:
+            copy.start()
+        for k in range(count):
+            first[k].wait()
+            second[k].start()
+        for copy in second:
+            copy.wait()
+
+    place = pl.BlockSpec(memory_space=pl.ANY)
+    return pl.pallas_call(
+        move,
+        out_shape=tuple(jax.ShapeDtypeStruct(r.shape, r.dtype) for r in results),
+        in_specs=[place] * count,
+        out_specs=(place,) * count,
+        scratch_shapes=[pltpu.VMEM(r.shape, r.dtype) for r in results]
+        + [pltpu.SemaphoreType.DMA((2, count))],
+        name="hand_over",
+    )(*results)
 
 
 def per_device(tokens, w_up, b_up, w_down, b_down, cotangent):
@@ -431,6 +482,7 @@
     half = width // 2
     unit = 2 * rows // NZ
     vmem = pl.BlockSpec(memory_space=pltpu.VMEM)
+    place = pl.BlockSpec(memory_space=pl.ANY)
     dma = pltpu.SemaphoreType.DMA
     scratch = [
         pltpu.VMEM((2, NC, 2, rows, feat), BF),
@@ -452,15 +504,23 @@
         pltpu.VMEM((4, 8, feat), F32),
         pltpu.VMEM((NZ, 2, 8, feat), F32),
         pltpu.VMEM((8, half), F32),
-        dma((2, NC, 8)), dma((2, NC, 8)),
-        dma((2, NC, 8)), dma((2, NC, 8)),
-        dma((2, NC)), dma((2, NC)),
-        dma((2, NC, NZ)), dma((2, NC, NZ)),
-        dma((2 * NC + 3,)), dma((2 * NC + 3,)),
-        dma((2, NC + 1)), dma((2, NC + 1)),
-        dma((9,)), dma((9,)),
+        pltpu.VMEM((feat, width), BF),
+        pltpu.VMEM((width, feat), BF),
+        pltpu.VMEM((feat, width), BF),
+        pltpu.VMEM((width, feat), BF),
+        dma((2, NC, 4)),
+        dma((2, NC, 4)),
+        dma((2, NC)),
+        dma((2, NC)),
+        dma((2 * NC + 1,)),
+        dma((2, NC + 1)),
+        dma((5,)),
+        dma((Z_POOL,)),
+        dma((X_POOL,)),
+        dma((POOL,)),
+        dma((4,)),
     ]
-    return pl.pallas_call(
+    results = pl.pallas_call(
         kernel,
         out_shape=(
             jax.ShapeDtypeStruct((rows, feat), BF),
@@ -470,14 +530,15 @@
             jax.ShapeDtypeStruct((width, feat), BF),
             jax.ShapeDtypeStruct((feat,), F32),
         ),
-        in_specs=[vmem] * 6,
-        out_specs=(vmem,) * 6,
+        in_specs=[vmem, place, vmem, place, vmem, vmem],
+        out_specs=(vmem, vmem, place, vmem, place, vmem),
         scratch_shapes=scratch,
         compiler_params=pltpu.CompilerParams(
             collective_id=0, has_side_effects=True, vmem_limit_bytes=60 * 2**20
         ),
         name="mlp_block",
     )(tokens, w_up, b_up, w_down, b_down, cotangent)
+    return hand_over(results)
 
 
 def solution(mesh):

time: 133 us -> 123 us (0.925)
  local copies, waits for them, and re-layouts: 7.48 us -> 0 us
  Pallas kernels: 125 us -> 122 us
    unnamed x12 -> x0, local copies, waits for them, and re-layouts: 7.48 us -> none
    pallas_call x1, Pallas kernels: 125 us -> 119 us  [per_device(): pl.pallas_call(kernel, out_shape=(jax.ShapeDtypeStruct((rows, feat), BF),...]
    pallas_call x0 -> x1, Pallas kernels: none -> 2.84 us  [hand_over(): pl.pallas_call(move, out_shape=tuple((jax.ShapeDtypeStruct(r.shape, r.dty...]
where the time goes in v4:
time: 123 us; the launch traced here: 122 us
  Pallas kernels  122 us (99%)
    pallas_call x1, Pallas kernels, per_device(): pl.pallas_call(kernel, out_shape=(jax.ShapeDtypeStruct((rows, feat), BF),...  119 us
    pallas_call x1, Pallas kernels, hand_over(): pl.pallas_call(move, out_shape=tuple((jax.ShapeDtypeStruct(r.shape, r.dty...  2.84 us

profile of v4, /device:TPU:1, one launch (start us, length us, event | category | flops | bytes accessed | tf_op | source)
XLA Modules:
  0.0 122.4 jit_solution(10503769267758013825)
XLA Ops:
  0.6 118.7 %mlp_block.1 = (bf16[64,384]{1,0:T(8,128)(2,1)}, bf16[64,384]{1,0:T(8,128)(2,1)}, bf16[384,1536]{1,0:T(8,128)(2,1)}, f32[384]{0:T(512)}, bf16[1536,384]{1,0:T(8,128)(2,1)}, /*index=5*/f32[384]{0:T(512)}) custom-call(bf16[64,384]{1,0:T(8,128)(2,1)} %tok_ref.1, bf16[384,1536]{1,0:T(8,128)(2,1)} %wup_hbm.1, f32[384]{0:T(512)} %bup_ref.1, ...), custom_call_target="tpu_custom_call" | custom-call | tf_op jit(solution)/shard_map/mlp_block/pallas_call | solution.py:523
  119.4 2.8 %hand_over.1 = (bf16[64,384]{1,0:T(8,128)(2,1)}, bf16[64,384]{1,0:T(8,128)(2,1)}, bf16[384,1536]{1,0:T(8,128)(2,1)}, f32[384]{0:T(512)}, bf16[1536,384]{1,0:T(8,128)(2,1)}, /*index=5*/f32[384]{0:T(512)}) custom-call(bf16[64,384]{1,0:T(8,128)(2,1)} %get-tuple-element.12.refs_0_, bf16[64,384]{1,0:T(8,128)(2,1)} %get-tuple-element.13.refs_1_, ...), custom_call_target="tpu_custom_call" | custom-call | tf_op jit(solution)/shard_map/hand_over/pallas_call | solution.py:468

commit v5 on v4

--- a/solution.py
+++ b/solution.py
@@ -15,44 +15,47 @@
 NC = len(CHUNKS)
 SIGN = (1, -1)
 PRE, GRAD = 0, 1
-Z_POOL, X_POOL, POOL = 64, 64, 32
-
-RS_X = ((1, 1, 0, 1, 1, 1, 0, 1), (0, 0, 1, 0, 1, 1, 0, 0))
-AG_X = ((1, 1, 0, 1, 0, 1, 1, 1), (1, 0, 0, 1, 1, 0, 1, 0))
+Z_POOL, X_POOL, POOL = 20, 20, 12
+
+RS_X = ((1, 0, 1, 1, 0, 1, 0, 1), (0, 1, 0, 1, 1, 1, 0, 0))
+AG_X = ((1, 0, 0, 1, 0, 0, 0, 0), (1, 1, 1, 1, 1, 1, 1, 1))
 ORDER = (
-    ("H", 0, 0), ("PP", 0, 1), ("PP", 0, 0), ("HF", 1, 0), ("HX", 0, 0), ("B1", 0, 0),
-    ("R2", 0, 1), ("PP", 1, 1), ("HF", 3, 0), ("PP", 1, 0), ("B2", 0, 0), ("PP", 7, 1),
-    ("R3", 0, 1), ("HF", 5, 0), ("PP", 3, 1), ("R1", 0, 0), ("B3", 0, 0), ("R2", 1, 1),
-    ("R2", 7, 1), ("HF", 2, 0), ("PP", 3, 0), ("R4", 0, 1), ("R2", 3, 1), ("R2", 0, 0),
-    ("HF", 4, 0), ("B4", 0, 0), ("PP", 2, 1), ("R1", 1, 0), ("R3", 1, 1), ("PP", 2, 0),
-    ("HF", 6, 0), ("R3", 7, 1), ("PP", 4, 1), ("R5", 0, 1), ("PP", 4, 0), ("R3", 3, 1),
-    ("R3", 0, 0), ("B5", 0, 0), ("R1", 3, 0), ("R2", 1, 0), ("PP", 5, 1), ("R4", 1, 1),
-    ("R2", 2, 0), ("PP", 5, 0), ("R4", 7, 1), ("PP", 6, 1), ("R4", 3, 1), ("R4", 0, 0),
-    ("R1", 2, 1), ("R3", 1, 0), ("R2", 3, 0), ("PP", 6, 0), ("R5", 1, 1), ("PP", 7, 0),
-    ("R3", 2, 0), ("R1", 4, 1), ("R5", 7, 1), ("R2", 6, 1), ("D", 0, 0), ("R5", 3, 1),
-    ("E", 0, 0), ("R4", 1, 0), ("R2", 2, 1), ("R3", 3, 0), ("R2", 6, 0), ("R1", 4, 0),
-    ("R4", 2, 0), ("R2", 4, 1), ("R3", 6, 1), ("A2", 0, 0), ("A2", 0, 1), ("R3", 2, 1),
-    ("R1", 5, 1), ("R4", 3, 0), ("R3", 6, 0), ("R2", 4, 0), ("R5", 2, 0), ("R3", 4, 1),
-    ("R4", 6, 1), ("R1", 5, 0), ("A3", 0, 0), ("A3", 0, 1), ("E", 1, 0), ("R4", 2, 1),
-    ("R2", 5, 1), ("R4", 6, 0), ("R3", 4, 0), ("R4", 4, 1), ("R1", 7, 0), ("R5", 6, 1),
-    ("E", 3, 0), ("A4", 0, 0), ("A4", 0, 1), ("R2", 5, 0), ("A2", 1, 0), ("R3", 5, 1),
-    ("R5", 6, 0), ("E", 2, 0), ("R4", 4, 0), ("R2", 7, 0), ("A2", 3, 0), ("A2", 3, 1),
-    ("A5", 0, 0), ("A5", 0, 1), ("A1", 1, 1), ("R3", 5, 0), ("A3", 1, 0), ("R4", 5, 1),
-    ("E", 4, 0), ("R3", 7, 0), ("A3", 3, 0), ("A3", 3, 1), ("A2", 1, 1), ("R4", 5, 0),
-    ("E", 6, 0), ("A4", 1, 0), ("A1", 2, 0), ("A1", 2, 1), ("A2", 4, 1), ("R4", 7, 0),
-    ("A4", 3, 0), ("A4", 3, 1), ("A3", 1, 1), ("F1", 0, 0), ("A2", 6, 0), ("A2", 6, 1),
-    ("A5", 1, 0), ("E", 5, 0), ("A1", 4, 0), ("A2", 2, 0), ("F2", 0, 0), ("A2", 2, 1),
-    ("A3", 4, 1), ("E", 7, 0), ("A5", 3, 0), ("A5", 3, 1), ("A4", 1, 1), ("A3", 6, 0),
-    ("A3", 6, 1), ("A2", 5, 0), ("A2", 4, 0), ("A3", 2, 0), ("A3", 2, 1), ("A4", 4, 1),
-    ("A2", 7, 0), ("F1", 1, 0), ("A4", 6, 0), ("A4", 6, 1), ("A3", 5, 0), ("A1", 5, 1),
-    ("C", 1, 0), ("W", 1, 0), ("A3", 4, 0), ("F2", 1, 0), ("F1", 3, 0), ("A5", 4, 1),
-    ("A4", 2, 0), ("A4", 2, 1), ("A1", 7, 1), ("A3", 7, 0), ("A5", 6, 0), ("W", 1, 1),
-    ("A5", 6, 1), ("A4", 5, 0), ("F2", 3, 0), ("A2", 5, 1), ("A4", 4, 0), ("F1", 2, 0),
-    ("A2", 7, 1), ("C", 3, 0), ("A5", 5, 0), ("A4", 7, 0), ("W", 3, 0), ("A3", 5, 1),
-    ("F2", 2, 0), ("F1", 4, 0), ("A3", 7, 1), ("A5", 7, 0), ("F1", 6, 0), ("A4", 5, 1),
-    ("F2", 4, 0), ("W", 3, 1), ("A4", 7, 1), ("F2", 6, 0), ("F1", 5, 0), ("F1", 7, 0),
-    ("C", 5, 0), ("F2", 5, 0), ("W", 5, 0), ("F2", 7, 0), ("FX", 0, 0), ("W", 5, 1),
-    ("C", 7, 0), ("W", 7, 0), ("W", 7, 1), ("END", 0, 0),
+    ("H", 0, 0), ("PP", 0, 1), ("PP", 0, 0), ("HX", 0, 0), ("HF", 1, 0), ("B1", 0, 0),
+    ("R2", 0, 1), ("PP", 7, 1), ("HF", 3, 0), ("B2", 0, 0), ("PP", 1, 1), ("PP", 1, 0),
+    ("R3", 0, 1), ("HF", 5, 0), ("PP", 3, 1), ("R1", 0, 0), ("B3", 0, 0), ("R2", 7, 1),
+    ("HF", 2, 0), ("R2", 1, 0), ("PP", 3, 0), ("R4", 0, 1), ("R2", 0, 0), ("PP", 2, 1),
+    ("HF", 4, 0), ("B4", 0, 0), ("PP", 2, 0), ("R1", 1, 1), ("R3", 1, 0), ("HF", 6, 0),
+    ("R3", 7, 1), ("PP", 4, 1), ("R5", 0, 1), ("R3", 0, 0), ("R2", 2, 1), ("PP", 4, 0),
+    ("R1", 3, 1), ("B5", 0, 0), ("R4", 1, 0), ("R2", 1, 1), ("PP", 5, 1), ("R4", 7, 1),
+    ("R4", 0, 0), ("PP", 5, 0), ("R3", 2, 1), ("PP", 6, 1), ("R1", 3, 0), ("R2", 3, 1),
+    ("R5", 1, 0), ("R2", 4, 0), ("R3", 1, 1), ("PP", 6, 0), ("R5", 7, 1), ("PP", 7, 0),
+    ("D", 0, 0), ("R1", 2, 0), ("R4", 2, 1), ("R2", 3, 0), ("R3", 3, 1), ("R2", 6, 1),
+    ("R3", 4, 0), ("R4", 1, 1), ("R2", 6, 0), ("R2", 2, 0), ("R1", 4, 1), ("R5", 2, 1),
+    ("E", 0, 0), ("R4", 3, 1), ("R3", 3, 0), ("R3", 6, 1), ("R4", 4, 0), ("R1", 5, 1),
+    ("R3", 6, 0), ("R3", 2, 0), ("R2", 4, 1), ("A2", 0, 0), ("A2", 0, 1), ("R4", 3, 0),
+    ("R1", 5, 0), ("R4", 6, 1), ("E", 1, 0), ("R5", 4, 0), ("R2", 5, 1), ("R4", 6, 0),
+    ("R4", 2, 0), ("R3", 4, 1), ("A3", 0, 0), ("A3", 0, 1), ("R1", 7, 0), ("E", 3, 0),
+    ("R5", 6, 1), ("R2", 5, 0), ("A2", 1, 1), ("R3", 5, 1), ("R5", 6, 0), ("E", 2, 0),
+    ("A1", 1, 0), ("R4", 4, 1), ("A4", 0, 0), ("A4", 0, 1), ("R2", 7, 0), ("A2", 3, 0),
+    ("A2", 3, 1), ("R3", 5, 0), ("A3", 1, 1), ("R4", 5, 1), ("A2", 2, 1), ("A2", 1, 0),
+    ("E", 6, 0), ("A1", 2, 0), ("A5", 0, 0), ("A5", 0, 1), ("R3", 7, 0), ("E", 4, 0),
+    ("A3", 3, 0), ("A3", 3, 1), ("R4", 5, 0), ("A4", 1, 1), ("A3", 2, 1), ("A3", 1, 0),
+    ("A2", 6, 1), ("A2", 2, 0), ("R4", 7, 0), ("A1", 6, 0), ("A2", 4, 1), ("A4", 3, 0),
+    ("F1", 0, 0), ("F1", 0, 1), ("A1", 4, 0), ("A5", 1, 1), ("E", 5, 0), ("A4", 2, 1),
+    ("A4", 1, 0), ("A4", 3, 1), ("F2", 0, 0), ("A3", 6, 1), ("F2", 0, 1), ("A3", 2, 0),
+    ("E", 7, 0), ("A2", 6, 0), ("A3", 4, 1), ("A5", 3, 0), ("A2", 4, 0), ("A2", 5, 1),
+    ("A5", 2, 1), ("F1", 1, 0), ("A5", 3, 1), ("W", 1, 1), ("A1", 5, 0), ("F1", 1, 1),
+    ("A4", 2, 0), ("A2", 7, 1), ("A4", 6, 1), ("F2", 1, 0), ("C", 1, 0), ("A3", 6, 0),
+    ("W", 1, 0), ("A4", 4, 1), ("F2", 1, 1), ("A3", 4, 0), ("A1", 7, 0), ("A3", 5, 1),
+    ("A2", 5, 0), ("F1", 2, 0), ("F1", 3, 0), ("A5", 6, 1), ("A3", 7, 1), ("W", 3, 1),
+    ("F1", 2, 1), ("F1", 3, 1), ("A5", 4, 1), ("A4", 4, 0), ("A4", 6, 0), ("F2", 2, 0),
+    ("F2", 3, 0), ("A2", 7, 0), ("F2", 2, 1), ("C", 3, 0), ("A4", 5, 1), ("F2", 3, 1),
+    ("W", 3, 0), ("A3", 5, 0), ("A4", 7, 1), ("F1", 4, 0), ("F1", 6, 1), ("F1", 6, 0),
+    ("A3", 7, 0), ("A5", 5, 1), ("F2", 4, 0), ("F1", 4, 1), ("F2", 6, 1), ("A4", 5, 0),
+    ("F2", 6, 0), ("A5", 7, 1), ("F2", 4, 1), ("A4", 7, 0), ("F1", 5, 1), ("F1", 5, 0),
+    ("F1", 7, 1), ("C", 5, 0), ("F1", 7, 0), ("F2", 5, 1), ("F2", 5, 0), ("C", 7, 0),
+    ("F2", 7, 1), ("FX", 0, 1), ("W", 5, 0), ("F2", 7, 0), ("FX", 0, 0), ("W", 5, 1),
+    ("W", 7, 0), ("W", 7, 1), ("END", 0, 0),
 )
 
 
@@ -74,19 +77,19 @@
 
 
 def kernel(
-    tok_ref, wup_hbm, bup_ref, wdn_hbm, bdn_ref, cot_ref,
+    tok_hbm, wup_hbm, bup_hbm, wdn_hbm, bdn_hbm, cot_hbm,
     out_ref, gtok_ref, gwu_hbm, gbu_ref, gwd_hbm, gbd_ref,
     tc, tct, part, zland, xland, own, full, acc_u, acc_d,
     opart, rcore, sy, ry, sx, rx, cs, bs, ball, brow,
-    wup_vm, wdn_vm, gwu_vm, gwd_vm,
-    rzr, azr, rxr, axr, hr, fr, bzr, zpool, xpool, pool, ls,
+    wup_vm, wdn_vm, bup_vm, bdn_vm, gwu_vm, gwd_vm,
+    zr, rxr, axr, hr, fr, bzr, zpool, xpool, pool, ls,
 ):
     gx, gy, gz = lax.axis_index("gx"), lax.axis_index("gy"), lax.axis_index("gz")
     z, xl = lax.rem(gz, NZ), lax.div(gz, NZ)
     xh, core = lax.div(gx, 2), lax.rem(gx, 2)
     feat, width = wup_vm.shape
     half = width // 2
-    rows = tok_ref.shape[0]
+    rows = tok_hbm.shape[0]
     crow = 2 * rows
     unit = crow // NZ
 
@@ -142,13 +145,13 @@
         return (
             rs_unit(op, c, zi(SIGN[d] * (5 - r)), shift, size),
             zland.at[op, c, d, r - 1, :, pl.ds(shift, size)],
-            rzr.at[op, c, r - 1], zdev[d],
+            zr.at[op, c, r % 2], zdev[d],
         )
 
     def rs_arrive(op, c, r):
         wide = half if RS_X[op][c] else width
         like = zland.at[op, c, :, r - 1, :, pl.ds(0, wide // 2 if r == 1 else wide)]
-        arrive_all(like, rzr.at[op, c, r - 1])
+        arrive_all(like, zr.at[op, c, r % 2])
 
     def rs_step(op, c, r):
         rs_arrive(op, c, r - 1)
@@ -179,12 +182,12 @@
         shift, size = (d * wide // 2, wide // 2) if r == 4 else (0, wide)
         cols = side(xl, shift, size) if AG_X[op][c] else pl.ds(shift, size)
         ref = full.at[op, c, t, :, cols]
-        return ref, ref, azr.at[op, c, r - 1], zdev[d]
+        return ref, ref, zr.at[op, c, r % 2], zdev[d]
 
     def ag_arrive(op, c, r):
         wide = half if AG_X[op][c] else width
         like = zland.at[op, c, :, 0, :, pl.ds(0, wide // 2 if r == 4 else wide)]
-        arrive_all(like, azr.at[op, c, r - 1])
+        arrive_all(like, zr.at[op, c, r % 2])
 
     def ag_x(op, c, j):
         ref = full.at[op, c, zi(j), :, mine]
@@ -216,21 +219,21 @@
         ref = tc.at[:, c, core]
         return h_copy(NC + c, ref, ref, coredev)
 
-    def f_core(c):
-        return opart.at[c, :, 1 - core], rcore.at[c], fr.at[0, c], coredev
-
-    def f_y(c):
-        return sy.at[c], ry.at[c], fr.at[1, c], ydev(CHUNKS[c][0])
-
-    def f_xh():
-        return sx, rx, fr.at[0, NC], xhdev
-
-    def ry_sum(h):
+    def f_core(c, op):
+        return opart.at[c, op, 1 - core], rcore.at[c, op], fr.at[0, op, c], coredev
+
+    def f_y(c, op):
+        return sy.at[c, op], ry.at[c, op], fr.at[1, op, c], ydev(CHUNKS[c][0])
+
+    def f_xh(op):
+        return sx.at[op], rx.at[op], fr.at[0, op, NC], xhdev
+
+    def ry_sum(h, op):
         picks = [c for c in range(NC) if CHUNKS[c][1] == h]
         for c in picks:
             if CHUNKS[c][0]:
-                arrive(f_y(c))
-        a, b, c, d = [ry[p].astype(F32) for p in picks]
+                arrive(f_y(c, op))
+        a, b, c, d = [ry[p, op].astype(F32) for p in picks]
         return (a + b) + (c + d)
 
     def b_y(d):
@@ -324,29 +327,27 @@
         start(ag_x(op, c, 4), xpool)
 
     def ev_F1(c, op):
-        for o in (PRE, GRAD):
-            if AG_X[o][c]:
-                arrive_all(xland.at[o, c], axr.at[o, c])
-            else:
-                ag_arrive(o, c, 4)
-        v = dot_nn(full[PRE, c].reshape(crow, width), wdn_vm[...])
-        opart[c, 0] = v.astype(BF).reshape(2, rows, feat)
-        v = dot_nt(full[GRAD, c].reshape(crow, width), wup_vm[...])
-        opart[c, 1] = v.astype(BF).reshape(2, rows, feat)
-        start(f_core(c), pool)
+        if AG_X[op][c]:
+            arrive_all(xland.at[op, c], axr.at[op, c])
+        else:
+            ag_arrive(op, c, 4)
+        left = full[op, c].reshape(crow, width)
+        v = dot_nn(left, wdn_vm[...]) if op == PRE else dot_nt(left, wup_vm[...])
+        opart[c, op] = v.astype(BF).reshape(2, rows, feat)
+        start(f_core(c, op), pool)
 
     def ev_F2(c, op):
-        arrive(f_core(c))
-        v = (opart[c, :, core].astype(F32) + rcore[c].astype(F32)).astype(BF)
+        arrive(f_core(c, op))
+        v = (opart[c, op, core].astype(F32) + rcore[c, op].astype(F32)).astype(BF)
         if CHUNKS[c][0]:
-            sy[c] = v
-            start(f_y(c), pool)
-        else:
-            ry[c] = v
+            sy[c, op] = v
+            start(f_y(c, op), pool)
+        else:
+            ry[c, op] = v
 
     def ev_FX(c, op):
-        sx[...] = ry_sum(1).astype(BF)
-        start(f_xh(), pool)
+        sx[op] = ry_sum(1, op).astype(BF)
+        start(f_xh(op), pool)
 
     def ev_W(c, op):
         p = c // 2
@@ -401,11 +402,14 @@
     def ev_END(c, op):
         arrive_all(bs.at[0:3], hr.at[2 * NC])
         gbu_ref[...] = jnp.sum(bs[lax.div(gz, 4)], axis=0)
-        total = ry_sum(0)
-        arrive(f_xh())
-        total += rx[...].astype(F32)
-        out_ref[...] = (total[0] + bdn_ref[...][None, :]).astype(BF)
-        gtok_ref[...] = total[1].astype(BF)
+        for o in (PRE, GRAD):
+            total = ry_sum(0, o)
+            arrive(f_xh(o))
+            total += rx[o].astype(F32)
+            if o == PRE:
+                out_ref[...] = (total + bdn_vm[...][None, :]).astype(BF)
+            else:
+                gtok_ref[...] = total.astype(BF)
 
     events = {
         "H": ev_H, "HX": ev_HX, "HF": ev_HF, "PP": ev_PP, "R1": ev_R1, "R5": ev_R5,
@@ -416,19 +420,20 @@
     def local(k):
         src, dst = (
             (wdn_hbm, wdn_vm), (wup_hbm, wup_vm), (gwu_vm, gwu_hbm), (gwd_vm, gwd_hbm),
+            (tok_hbm, tc.at[0, 0, core]), (cot_hbm, tc.at[1, 0, core]),
+            (bup_hbm, bup_vm), (bdn_hbm, bdn_vm),
         )[k]
         return pltpu.make_async_copy(src, dst, ls.at[k])
 
-    local(0).start()
-    local(1).start()
-    for i, ref in enumerate((tok_ref, cot_ref)):
-        tc[i, 0, core] = ref[...]
-    ball[z, xl] = jnp.broadcast_to(bup_ref[...][None, :], ball.shape[2:])
-
+    for k in (4, 5, 6, 7, 0, 1):
+        local(k).start()
     barrier = pltpu.get_barrier_semaphore()
     peers = (zdev[0], zdev[1], xdev, coredev, xhdev, ydev(1), ydev(2), ydev(3))
     for dev in peers:
         pl.semaphore_signal(barrier, inc=1, device_id=dev, device_id_type=MESH)
+    for k in (4, 5, 6, 7):
+        local(k).wait()
+    ball[z, xl] = jnp.broadcast_to(bup_vm[...][None, :], ball.shape[2:])
     pl.semaphore_wait(barrier, len(peers))
 
     for kind, c, op in ORDER:
@@ -450,19 +455,31 @@
 
 def hand_over(results):
     count = len(results)
+    pieces = []
+    for k, r in enumerate(results):
+        parts = 4 if r.size > 2**18 else 1
+        size = r.shape[0] // parts
+        pieces += [(k, i * size, size) for i in range(parts)]
 
     def move(*refs):
         source, target, held = refs[:count], refs[count:2 * count], refs[2 * count:3 * count]
         sems = refs[3 * count]
-        first = [pltpu.make_async_copy(source[k], held[k], sems.at[0, k]) for k in range(count)]
-        second = [pltpu.make_async_copy(held[k], target[k], sems.at[1, k]) for k in range(count)]
-        for copy in first:
-            copy.start()
-        for k in range(count):
-            first[k].wait()
-            second[k].start()
-        for copy in second:
-            copy.wait()
+
+        def copy(side, i):
+            k, at, size = pieces[i]
+            ends = (source[k], held[k], target[k])
+            rows = pl.ds(at, size)
+            return pltpu.make_async_copy(
+                ends[side].at[rows], ends[side + 1].at[rows], sems.at[side, i]
+            )
+
+        for i in range(len(pieces)):
+            copy(0, i).start()
+        for i in range(len(pieces)):
+            copy(0, i).wait()
+            copy(1, i).start()
+        for i in range(len(pieces)):
+            copy(1, i).wait()
 
     place = pl.BlockSpec(memory_space=pl.ANY)
     return pl.pallas_call(
@@ -471,7 +488,7 @@
         in_specs=[place] * count,
         out_specs=(place,) * count,
         scratch_shapes=[pltpu.VMEM(r.shape, r.dtype) for r in results]
-        + [pltpu.SemaphoreType.DMA((2, count))],
+        + [pltpu.SemaphoreType.DMA((2, len(pieces)))],
         name="hand_over",
     )(*results)
 
@@ -506,19 +523,20 @@
         pltpu.VMEM((8, half), F32),
         pltpu.VMEM((feat, width), BF),
         pltpu.VMEM((width, feat), BF),
+        pltpu.VMEM((feat,), F32),
+        pltpu.VMEM((feat,), F32),
         pltpu.VMEM((feat, width), BF),
         pltpu.VMEM((width, feat), BF),
-        dma((2, NC, 4)),
-        dma((2, NC, 4)),
+        dma((2, NC, 2)),
         dma((2, NC)),
         dma((2, NC)),
         dma((2 * NC + 1,)),
-        dma((2, NC + 1)),
+        dma((2, 2, NC + 1)),
         dma((5,)),
         dma((Z_POOL,)),
         dma((X_POOL,)),
         dma((POOL,)),
-        dma((4,)),
+        dma((8,)),
     ]
     results = pl.pallas_call(
         kernel,
@@ -530,7 +548,7 @@
             jax.ShapeDtypeStruct((width, feat), BF),
             jax.ShapeDtypeStruct((feat,), F32),
         ),
-        in_specs=[vmem, place, vmem, place, vmem, vmem],
+        in_specs=[place] * 6,
         out_specs=(vmem, vmem, place, vmem, place, vmem),
         scratch_shapes=scratch,
         compiler_params=pltpu.CompilerParams(

time: 123 us -> 119 us (0.967)
  Pallas kernels: 122 us -> 118 us
    pallas_call x1, Pallas kernels: 119 us -> 115 us  [per_device(): pl.pallas_call(kernel, out_shape=(jax.ShapeDtypeStruct((rows, feat), BF),...]
where the time goes in v5:
time: 119 us
  Pallas kernels  118 us (99%)
    pallas_call x1, Pallas kernels, per_device(): pl.pallas_call(kernel, out_shape=(jax.ShapeDtypeStruct((rows, feat), BF),...  115 us
    pallas_call x1, Pallas kernels, hand_over(): pl.pallas_call(move, out_shape=tuple((jax.ShapeDtypeStruct(r.shape, r.dty...  2.63 us

profile of v5, /device:TPU:1, one launch (start us, length us, event | category | flops | bytes accessed | tf_op | source)
XLA Modules:
  0.0 118.7 jit_solution(10403066249658228297)
XLA Ops:
  0.6 115.3 %mlp_block.1 = (bf16[64,384]{1,0:T(8,128)(2,1)}, bf16[64,384]{1,0:T(8,128)(2,1)}, bf16[384,1536]{1,0:T(8,128)(2,1)}, f32[384]{0:T(512)}, bf16[1536,384]{1,0:T(8,128)(2,1)}, /*index=5*/f32[384]{0:T(512)}) custom-call(bf16[64,384]{1,0:T(8,128)(2,1)} %tok_hbm.1, bf16[384,1536]{1,0:T(8,128)(2,1)} %wup_hbm.1, f32[384]{0:T(512)} %bup_hbm.1, ...), custom_call_target="tpu_custom_call" | custom-call | tf_op jit(solution)/shard_map/mlp_block/pallas_call | solution.py:541
  115.9 2.6 %hand_over.1 = (bf16[64,384]{1,0:T(8,128)(2,1)}, bf16[64,384]{1,0:T(8,128)(2,1)}, bf16[384,1536]{1,0:T(8,128)(2,1)}, f32[384]{0:T(512)}, bf16[1536,384]{1,0:T(8,128)(2,1)}, /*index=5*/f32[384]{0:T(512)}) custom-call(bf16[64,384]{1,0:T(8,128)(2,1)} %get-tuple-element.12.refs_0_, bf16[64,384]{1,0:T(8,128)(2,1)} %get-tuple-element.13.refs_1_, ...), custom_call_target="tpu_custom_call" | custom-call | tf_op jit(solution)/shard_map/hand_over/pallas_call | solution.py:485

commit v6 on v5

--- a/solution.py
+++ b/solution.py
@@ -17,45 +17,45 @@
 PRE, GRAD = 0, 1
 Z_POOL, X_POOL, POOL = 20, 20, 12
 
-RS_X = ((1, 0, 1, 1, 0, 1, 0, 1), (0, 1, 0, 1, 1, 1, 0, 0))
-AG_X = ((1, 0, 0, 1, 0, 0, 0, 0), (1, 1, 1, 1, 1, 1, 1, 1))
+RS_X = ((1, 1, 1, 0, 1, 1, 0, 1), (0, 0, 1, 0, 1, 0, 0, 1))
+AG_X = ((1, 1, 1, 1, 0, 0, 1, 0), (1, 1, 0, 0, 1, 1, 0, 1))
 ORDER = (
-    ("H", 0, 0), ("PP", 0, 1), ("PP", 0, 0), ("HX", 0, 0), ("HF", 1, 0), ("B1", 0, 0),
-    ("R2", 0, 1), ("PP", 7, 1), ("HF", 3, 0), ("B2", 0, 0), ("PP", 1, 1), ("PP", 1, 0),
-    ("R3", 0, 1), ("HF", 5, 0), ("PP", 3, 1), ("R1", 0, 0), ("B3", 0, 0), ("R2", 7, 1),
-    ("HF", 2, 0), ("R2", 1, 0), ("PP", 3, 0), ("R4", 0, 1), ("R2", 0, 0), ("PP", 2, 1),
-    ("HF", 4, 0), ("B4", 0, 0), ("PP", 2, 0), ("R1", 1, 1), ("R3", 1, 0), ("HF", 6, 0),
-    ("R3", 7, 1), ("PP", 4, 1), ("R5", 0, 1), ("R3", 0, 0), ("R2", 2, 1), ("PP", 4, 0),
-    ("R1", 3, 1), ("B5", 0, 0), ("R4", 1, 0), ("R2", 1, 1), ("PP", 5, 1), ("R4", 7, 1),
-    ("R4", 0, 0), ("PP", 5, 0), ("R3", 2, 1), ("PP", 6, 1), ("R1", 3, 0), ("R2", 3, 1),
-    ("R5", 1, 0), ("R2", 4, 0), ("R3", 1, 1), ("PP", 6, 0), ("R5", 7, 1), ("PP", 7, 0),
-    ("D", 0, 0), ("R1", 2, 0), ("R4", 2, 1), ("R2", 3, 0), ("R3", 3, 1), ("R2", 6, 1),
-    ("R3", 4, 0), ("R4", 1, 1), ("R2", 6, 0), ("R2", 2, 0), ("R1", 4, 1), ("R5", 2, 1),
-    ("E", 0, 0), ("R4", 3, 1), ("R3", 3, 0), ("R3", 6, 1), ("R4", 4, 0), ("R1", 5, 1),
-    ("R3", 6, 0), ("R3", 2, 0), ("R2", 4, 1), ("A2", 0, 0), ("A2", 0, 1), ("R4", 3, 0),
-    ("R1", 5, 0), ("R4", 6, 1), ("E", 1, 0), ("R5", 4, 0), ("R2", 5, 1), ("R4", 6, 0),
-    ("R4", 2, 0), ("R3", 4, 1), ("A3", 0, 0), ("A3", 0, 1), ("R1", 7, 0), ("E", 3, 0),
-    ("R5", 6, 1), ("R2", 5, 0), ("A2", 1, 1), ("R3", 5, 1), ("R5", 6, 0), ("E", 2, 0),
-    ("A1", 1, 0), ("R4", 4, 1), ("A4", 0, 0), ("A4", 0, 1), ("R2", 7, 0), ("A2", 3, 0),
-    ("A2", 3, 1), ("R3", 5, 0), ("A3", 1, 1), ("R4", 5, 1), ("A2", 2, 1), ("A2", 1, 0),
-    ("E", 6, 0), ("A1", 2, 0), ("A5", 0, 0), ("A5", 0, 1), ("R3", 7, 0), ("E", 4, 0),
-    ("A3", 3, 0), ("A3", 3, 1), ("R4", 5, 0), ("A4", 1, 1), ("A3", 2, 1), ("A3", 1, 0),
-    ("A2", 6, 1), ("A2", 2, 0), ("R4", 7, 0), ("A1", 6, 0), ("A2", 4, 1), ("A4", 3, 0),
-    ("F1", 0, 0), ("F1", 0, 1), ("A1", 4, 0), ("A5", 1, 1), ("E", 5, 0), ("A4", 2, 1),
-    ("A4", 1, 0), ("A4", 3, 1), ("F2", 0, 0), ("A3", 6, 1), ("F2", 0, 1), ("A3", 2, 0),
-    ("E", 7, 0), ("A2", 6, 0), ("A3", 4, 1), ("A5", 3, 0), ("A2", 4, 0), ("A2", 5, 1),
-    ("A5", 2, 1), ("F1", 1, 0), ("A5", 3, 1), ("W", 1, 1), ("A1", 5, 0), ("F1", 1, 1),
-    ("A4", 2, 0), ("A2", 7, 1), ("A4", 6, 1), ("F2", 1, 0), ("C", 1, 0), ("A3", 6, 0),
-    ("W", 1, 0), ("A4", 4, 1), ("F2", 1, 1), ("A3", 4, 0), ("A1", 7, 0), ("A3", 5, 1),
-    ("A2", 5, 0), ("F1", 2, 0), ("F1", 3, 0), ("A5", 6, 1), ("A3", 7, 1), ("W", 3, 1),
-    ("F1", 2, 1), ("F1", 3, 1), ("A5", 4, 1), ("A4", 4, 0), ("A4", 6, 0), ("F2", 2, 0),
-    ("F2", 3, 0), ("A2", 7, 0), ("F2", 2, 1), ("C", 3, 0), ("A4", 5, 1), ("F2", 3, 1),
-    ("W", 3, 0), ("A3", 5, 0), ("A4", 7, 1), ("F1", 4, 0), ("F1", 6, 1), ("F1", 6, 0),
-    ("A3", 7, 0), ("A5", 5, 1), ("F2", 4, 0), ("F1", 4, 1), ("F2", 6, 1), ("A4", 5, 0),
-    ("F2", 6, 0), ("A5", 7, 1), ("F2", 4, 1), ("A4", 7, 0), ("F1", 5, 1), ("F1", 5, 0),
-    ("F1", 7, 1), ("C", 5, 0), ("F1", 7, 0), ("F2", 5, 1), ("F2", 5, 0), ("C", 7, 0),
-    ("F2", 7, 1), ("FX", 0, 1), ("W", 5, 0), ("F2", 7, 0), ("FX", 0, 0), ("W", 5, 1),
-    ("W", 7, 0), ("W", 7, 1), ("END", 0, 0),
+    ("H", 0, 0), ("PP", 0, 0), ("PP", 0, 1), ("HX", 0, 0), ("HF", 1, 0), ("B1", 0, 0),
+    ("R2", 0, 1), ("PP", 7, 0), ("HF", 3, 0), ("PP", 1, 1), ("PP", 1, 0), ("B2", 0, 0),
+    ("PP", 3, 0), ("R1", 0, 0), ("HF", 5, 0), ("R3", 0, 1), ("PP", 3, 1), ("HF", 2, 0),
+    ("R2", 1, 1), ("B3", 0, 0), ("PP", 5, 1), ("R2", 3, 0), ("R2", 0, 0), ("HF", 4, 0),
+    ("PP", 2, 0), ("R4", 0, 1), ("R2", 3, 1), ("R1", 7, 0), ("HF", 6, 0), ("R3", 1, 1),
+    ("PP", 2, 1), ("B4", 0, 0), ("R2", 5, 1), ("PP", 4, 0), ("R3", 3, 0), ("R1", 1, 0),
+    ("R3", 0, 0), ("PP", 4, 1), ("R5", 0, 1), ("PP", 5, 0), ("R3", 3, 1), ("R2", 7, 0),
+    ("PP", 6, 0), ("B5", 0, 0), ("R4", 1, 1), ("R1", 2, 0), ("R3", 5, 1), ("PP", 7, 1),
+    ("R4", 3, 0), ("R2", 1, 0), ("R4", 0, 0), ("PP", 6, 1), ("R4", 3, 1), ("D", 0, 0),
+    ("R1", 2, 1), ("R2", 6, 0), ("R3", 7, 0), ("R5", 1, 1), ("R2", 2, 0), ("R4", 5, 1),
+    ("R5", 3, 0), ("R1", 4, 0), ("R3", 1, 0), ("R2", 6, 1), ("R5", 3, 1), ("R2", 2, 1),
+    ("R3", 6, 0), ("R4", 7, 0), ("R1", 4, 1), ("E", 0, 0), ("R3", 2, 0), ("R2", 4, 0),
+    ("R5", 5, 1), ("R4", 1, 0), ("R3", 6, 1), ("R3", 2, 1), ("R4", 6, 0), ("R1", 5, 0),
+    ("R2", 4, 1), ("A2", 0, 0), ("A2", 0, 1), ("R4", 2, 0), ("R3", 4, 0), ("R1", 7, 1),
+    ("E", 1, 0), ("R4", 2, 1), ("E", 3, 0), ("R4", 6, 1), ("R3", 4, 1), ("A3", 0, 0),
+    ("R2", 5, 0), ("A3", 0, 1), ("R5", 6, 0), ("R4", 4, 0), ("R2", 7, 1), ("A2", 1, 0),
+    ("A2", 1, 1), ("E", 2, 0), ("A2", 3, 0), ("A1", 3, 1), ("R5", 6, 1), ("R4", 4, 1),
+    ("A4", 0, 0), ("R3", 5, 0), ("A4", 0, 1), ("R3", 7, 1), ("A3", 1, 0), ("A3", 1, 1),
+    ("A2", 2, 0), ("A3", 3, 0), ("A1", 2, 1), ("A2", 3, 1), ("E", 4, 0), ("A5", 0, 0),
+    ("E", 6, 0), ("R4", 7, 1), ("A5", 0, 1), ("R4", 5, 0), ("A4", 1, 0), ("A4", 1, 1),
+    ("A3", 2, 0), ("A4", 3, 0), ("A2", 2, 1), ("A3", 3, 1), ("A2", 4, 1), ("A2", 6, 0),
+    ("A1", 4, 0), ("E", 7, 0), ("E", 5, 0), ("F1", 0, 0), ("A5", 1, 1), ("A5", 3, 0),
+    ("A5", 1, 0), ("F1", 0, 1), ("A3", 2, 1), ("F2", 0, 0), ("A4", 2, 0), ("A1", 6, 1),
+    ("A4", 3, 1), ("F2", 0, 1), ("A3", 4, 1), ("A3", 6, 0), ("A2", 4, 0), ("A2", 7, 1),
+    ("A2", 5, 1), ("A4", 2, 1), ("A5", 2, 0), ("A1", 7, 0), ("A2", 6, 1), ("F1", 3, 1),
+    ("A4", 4, 1), ("A1", 5, 0), ("A4", 6, 0), ("F1", 1, 1), ("C", 1, 0), ("A3", 4, 0),
+    ("F1", 1, 0), ("A3", 7, 1), ("F1", 3, 0), ("F1", 2, 1), ("F2", 1, 0), ("C", 3, 0),
+    ("A2", 7, 0), ("F2", 1, 1), ("F2", 3, 1), ("A3", 6, 1), ("F2", 2, 1), ("A5", 4, 1),
+    ("F2", 3, 0), ("A3", 5, 1), ("W", 1, 1), ("A2", 5, 0), ("A5", 6, 0), ("W", 1, 0),
+    ("A4", 4, 0), ("A4", 7, 1), ("F1", 2, 0), ("W", 3, 1), ("A3", 7, 0), ("W", 3, 0),
+    ("A4", 5, 1), ("F2", 2, 0), ("A4", 6, 1), ("F1", 4, 1), ("A3", 5, 0), ("F1", 4, 0),
+    ("A5", 7, 1), ("F1", 6, 0), ("F2", 4, 1), ("A4", 7, 0), ("A5", 5, 1), ("F2", 4, 0),
+    ("F1", 6, 1), ("F2", 6, 0), ("A4", 5, 0), ("F1", 7, 1), ("F2", 6, 1), ("F1", 5, 1),
+    ("C", 5, 0), ("F1", 7, 0), ("F2", 7, 1), ("C", 7, 0), ("F1", 5, 0), ("F2", 7, 0),
+    ("FX", 0, 0), ("F2", 5, 1), ("W", 5, 0), ("FX", 0, 1), ("F2", 5, 0), ("W", 7, 0),
+    ("W", 5, 1), ("W", 7, 1), ("END", 0, 0),
 )
 
 
@@ -78,10 +78,11 @@
 
 def kernel(
     tok_hbm, wup_hbm, bup_hbm, wdn_hbm, bdn_hbm, cot_hbm,
-    out_ref, gtok_ref, gwu_hbm, gbu_ref, gwd_hbm, gbd_ref,
+    out_hbm, gtok_hbm, gwu_hbm, gbu_hbm, gwd_hbm, gbd_hbm,
     tc, tct, part, zland, xland, own, full, acc_u, acc_d,
     opart, rcore, sy, ry, sx, rx, cs, bs, ball, brow,
     wup_vm, wdn_vm, bup_vm, bdn_vm, gwu_vm, gwd_vm,
+    out_vm, gtok_vm, gbu_vm, gbd_vm,
     zr, rxr, axr, hr, fr, bzr, zpool, xpool, pool, ls,
 ):
     gx, gy, gz = lax.axis_index("gx"), lax.axis_index("gy"), lax.axis_index("gz")
@@ -384,7 +385,8 @@
                 start(b_y(d), pool)
 
     def ev_D(c, op):
-        gbd_ref[...] = jnp.sum(tc[1].reshape(NC * crow, feat).astype(F32), axis=0)
+        gbd_vm[...] = jnp.sum(tc[1].reshape(NC * crow, feat).astype(F32), axis=0)
+        local(11).start()
 
     def bias_step(r):
         if r == 1:
@@ -401,15 +403,17 @@
 
     def ev_END(c, op):
         arrive_all(bs.at[0:3], hr.at[2 * NC])
-        gbu_ref[...] = jnp.sum(bs[lax.div(gz, 4)], axis=0)
+        gbu_vm[...] = jnp.sum(bs[lax.div(gz, 4)], axis=0)
+        local(10).start()
         for o in (PRE, GRAD):
             total = ry_sum(0, o)
             arrive(f_xh(o))
             total += rx[o].astype(F32)
             if o == PRE:
-                out_ref[...] = (total + bdn_vm[...][None, :]).astype(BF)
+                out_vm[...] = (total + bdn_vm[...][None, :]).astype(BF)
             else:
-                gtok_ref[...] = total.astype(BF)
+                gtok_vm[...] = total.astype(BF)
+            local(8 + o).start()
 
     events = {
         "H": ev_H, "HX": ev_HX, "HF": ev_HF, "PP": ev_PP, "R1": ev_R1, "R5": ev_R5,
@@ -421,7 +425,8 @@
         src, dst = (
             (wdn_hbm, wdn_vm), (wup_hbm, wup_vm), (gwu_vm, gwu_hbm), (gwd_vm, gwd_hbm),
             (tok_hbm, tc.at[0, 0, core]), (cot_hbm, tc.at[1, 0, core]),
-            (bup_hbm, bup_vm), (bdn_hbm, bdn_vm),
+            (bup_hbm, bup_vm), (bdn_hbm, bdn_vm), (out_vm, out_hbm), (gtok_vm, gtok_hbm),
+            (gbu_vm, gbu_hbm), (gbd_vm, gbd_hbm),
         )[k]
         return pltpu.make_async_copy(src, dst, ls.at[k])
 
@@ -449,8 +454,8 @@
         for copy in held:
             if copy is not None:
                 copy.wait_send()
-    local(2).wait()
-    local(3).wait()
+    for k in (2, 3, 8, 9, 10, 11):
+        local(k).wait()
 
 
 def hand_over(results):
@@ -498,7 +503,6 @@
     width = w_up.shape[1]
     half = width // 2
     unit = 2 * rows // NZ
-    vmem = pl.BlockSpec(memory_space=pltpu.VMEM)
     place = pl.BlockSpec(memory_space=pl.ANY)
     dma = pltpu.SemaphoreType.DMA
     scratch = [
@@ -527,6 +531,10 @@
         pltpu.VMEM((feat,), F32),
         pltpu.VMEM((feat, width), BF),
         pltpu.VMEM((width, feat), BF),
+        pltpu.VMEM((rows, feat), BF),
+        pltpu.VMEM((rows, feat), BF),
+        pltpu.VMEM((feat,), F32),
+        pltpu.VMEM((feat,), F32),
         dma((2, NC, 2)),
         dma((2, NC)),
         dma((2, NC)),
@@ -536,7 +544,7 @@
         dma((Z_POOL,)),
         dma((X_POOL,)),
         dma((POOL,)),
-        dma((8,)),
+        dma((12,)),
     ]
     results = pl.pallas_call(
         kernel,
@@ -549,7 +557,7 @@
             jax.ShapeDtypeStruct((feat,), F32),
         ),
         in_specs=[place] * 6,
-        out_specs=(vmem, vmem, place, vmem, place, vmem),
+        out_specs=(place,) * 6,
         scratch_shapes=scratch,
         compiler_params=pltpu.CompilerParams(
             collective_id=0, has_side_effects=True, vmem_limit_bytes=60 * 2**20

time: 119 us -> 117 us (0.983)
  Pallas kernels: 118 us -> 116 us
    pallas_call x1, Pallas kernels: 115 us -> 113 us  [per_device(): pl.pallas_call(kernel, out_shape=(jax.ShapeDtypeStruct((rows, feat), BF),...]
where the time goes in v6:
time: 117 us; the launch traced here: 116 us
  Pallas kernels  116 us (99%)
    pallas_call x1, Pallas kernels, per_device(): pl.pallas_call(kernel, out_shape=(jax.ShapeDtypeStruct((rows, feat), BF),...  113 us
    pallas_call x1, Pallas kernels, hand_over(): pl.pallas_call(move, out_shape=tuple((jax.ShapeDtypeStruct(r.shape, r.dty...  2.63 us

profile of v6, /device:TPU:1, one launch (start us, length us, event | category | flops | bytes accessed | tf_op | source)
XLA Modules:
  0.0 116.5 jit_solution(5883645889607325884)
XLA Ops:
  0.6 113.0 %mlp_block.1 = (bf16[64,384]{1,0:T(8,128)(2,1)}, bf16[64,384]{1,0:T(8,128)(2,1)}, bf16[384,1536]{1,0:T(8,128)(2,1)}, f32[384]{0:T(512)}, bf16[1536,384]{1,0:T(8,128)(2,1)}, /*index=5*/f32[384]{0:T(512)}) custom-call(bf16[64,384]{1,0:T(8,128)(2,1)} %tok_hbm.1, bf16[384,1536]{1,0:T(8,128)(2,1)} %wup_hbm.1, f32[384]{0:T(512)} %bup_hbm.1, ...), custom_call_target="tpu_custom_call" | custom-call | tf_op jit(solution)/shard_map/mlp_block/pallas_call | solution.py:549
  113.7 2.6 %hand_over.1 = (bf16[64,384]{1,0:T(8,128)(2,1)}, bf16[64,384]{1,0:T(8,128)(2,1)}, bf16[384,1536]{1,0:T(8,128)(2,1)}, f32[384]{0:T(512)}, bf16[1536,384]{1,0:T(8,128)(2,1)}, /*index=5*/f32[384]{0:T(512)}) custom-call(bf16[64,384]{1,0:T(8,128)(2,1)} %get-tuple-element.12.refs_0_, bf16[64,384]{1,0:T(8,128)(2,1)} %get-tuple-element.13.refs_1_, ...), custom_call_target="tpu_custom_call" | custom-call | tf_op jit(solution)/shard_map/hand_over/pallas_call | solution.py:490

commit v7 on v6

--- a/solution.py
+++ b/solution.py
@@ -302,7 +302,7 @@
             else:
                 arrive(rs_x(o, c))
                 got.append(own[o, c] + xland[o, c, 0].astype(F32))
-        value, slope = gelu_both(got[PRE] + brow[0:1, :])
+        value, slope = gelu_both(got[PRE] + brow[...])
         full[PRE, c, z, :, mine] = value.astype(BF)
         full[GRAD, c, z, :, mine] = (got[GRAD] * slope).astype(BF)
         for o in (PRE, GRAD):
@@ -430,15 +430,15 @@
         )[k]
         return pltpu.make_async_copy(src, dst, ls.at[k])
 
-    for k in (4, 5, 6, 7, 0, 1):
-        local(k).start()
     barrier = pltpu.get_barrier_semaphore()
     peers = (zdev[0], zdev[1], xdev, coredev, xhdev, ydev(1), ydev(2), ydev(3))
     for dev in peers:
         pl.semaphore_signal(barrier, inc=1, device_id=dev, device_id_type=MESH)
+    for k in (4, 5, 6, 7, 0, 1):
+        local(k).start()
     for k in (4, 5, 6, 7):
         local(k).wait()
-    ball[z, xl] = jnp.broadcast_to(bup_vm[...][None, :], ball.shape[2:])
+    ball[z, xl] = bup_vm[...][None, :]
     pl.semaphore_wait(barrier, len(peers))
 
     for kind, c, op in ORDER:
@@ -523,8 +523,8 @@
         pltpu.VMEM((2, rows, feat), BF),
         pltpu.VMEM((8, width), F32),
         pltpu.VMEM((4, 8, feat), F32),
-        pltpu.VMEM((NZ, 2, 8, feat), F32),
-        pltpu.VMEM((8, half), F32),
+        pltpu.VMEM((NZ, 2, 1, feat), F32),
+        pltpu.VMEM((1, half), F32),
         pltpu.VMEM((feat, width), BF),
         pltpu.VMEM((width, feat), BF),
         pltpu.VMEM((feat,), F32),

time: 117 us -> 116 us (level)
  no operation moved by 1% of the time
where the time goes in v7:
time: 116 us
  Pallas kernels  115 us (99%)
    pallas_call x1, Pallas kernels, per_device(): pl.pallas_call(kernel, out_shape=(jax.ShapeDtypeStruct((rows, feat), BF),...  112 us
    pallas_call x1, Pallas kernels, hand_over(): pl.pallas_call(move, out_shape=tuple((jax.ShapeDtypeStruct(r.shape, r.dty...  2.63 us

profile of v7, /device:TPU:1, one launch (start us, length us, event | category | flops | bytes accessed | tf_op | source)
XLA Modules:
  0.0 115.7 jit_solution(2554565696960946844)
XLA Ops:
  0.6 112.2 %mlp_block.1 = (bf16[64,384]{1,0:T(8,128)(2,1)}, bf16[64,384]{1,0:T(8,128)(2,1)}, bf16[384,1536]{1,0:T(8,128)(2,1)}, f32[384]{0:T(512)}, bf16[1536,384]{1,0:T(8,128)(2,1)}, /*index=5*/f32[384]{0:T(512)}) custom-call(bf16[64,384]{1,0:T(8,128)(2,1)} %tok_hbm.1, bf16[384,1536]{1,0:T(8,128)(2,1)} %wup_hbm.1, f32[384]{0:T(512)} %bup_hbm.1, ...), custom_call_target="tpu_custom_call" | custom-call | tf_op jit(solution)/shard_map/mlp_block/pallas_call | solution.py:549
  112.9 2.6 %hand_over.1 = (bf16[64,384]{1,0:T(8,128)(2,1)}, bf16[64,384]{1,0:T(8,128)(2,1)}, bf16[384,1536]{1,0:T(8,128)(2,1)}, f32[384]{0:T(512)}, bf16[1536,384]{1,0:T(8,128)(2,1)}, /*index=5*/f32[384]{0:T(512)}) custom-call(bf16[64,384]{1,0:T(8,128)(2,1)} %get-tuple-element.12.refs_0_, bf16[64,384]{1,0:T(8,128)(2,1)} %get-tuple-element.13.refs_1_, ...), custom_call_target="tpu_custom_call" | custom-call | tf_op jit(solution)/shard_map/hand_over/pallas_call | solution.py:490
